TPU v7x, 32 devices: a whole 2x2x4 slice. The times are simulated.
32 devices in a mesh: group: 16 (over z, y, core), tensor: 2 (over x).
Axes of the slice: x: 2, y: 2, z: 4, core: 2. Of those that a mesh axis runs over, the one named last changes fastest.
Arguments:
- new_q: bfloat16 [8192, 5120], P('group', 'tensor'), may hold values from -420 to 420
- new_k: bfloat16 [8192, 5120], P('group', 'tensor'), may hold values from -420 to 420
- new_v: bfloat16 [8192, 5120], P('group', 'tensor'), may hold values from -6 to 6
- cache_k: bfloat16 [14336, 5120], P('group', 'tensor'), may hold values from -30 to 30
- cache_v: bfloat16 [14336, 5120], P('group', 'tensor'), may hold values from -6 to 6
- q_gain: float32 [5120], P('tensor'), may hold values from 1 to 3
- k_gain: float32 [5120], P('tensor'), may hold values from 1 to 3
- cache_len: int32 [16], replicated, may hold values from 2 to 1664, as said below
- home_blocks: int32 [16], replicated, may hold values from 1 to 7, as said below
Outputs:
- attended: bfloat16 [8192, 5120], P('group', 'tensor')
Inputs may be any that keep to these rules, and one draw needn't show every extreme that they name: ceil(cache_len / 128) of a request and of its partner (index XOR 1) sum to at most 14. home_blocks[r] = min(ceil(cache_len[r] / 128), 7).
All inputs are finite; a program needn't handle non-finite values.
Results may differ from a plain program's by a relative error of at most 0.03.
Values may be sent and summed in bfloat16 or wider, within the bound.
No kernel may reach another device: no remote copies, remote signals or barrier semaphores. Data moves between devices by JAX's collectives and lax.ppermute only.
A program may use at most 192 MiB of HBM per device.

v0:
```python
import jax
import jax.numpy as jnp
from jax import lax
from jax.sharding import PartitionSpec as P

HEADS = 40
HD = 128
CB = 128


NEGATIVE = -1e30


def swapped(value, axis, bit):
    mask = 2**bit
    pairs = [(source, source ^ mask) for source in range(lax.axis_size(axis))]
    return lax.ppermute(value, axis, pairs)


def partial_block(queries, key_block, value_block, usable):
    scores = jnp.einsum(
        "qhd,khd->qhk", queries, key_block, preferred_element_type=jnp.float32
    ) * HD ** (-0.5)
    scores = jnp.where(usable[None, None, :], scores, NEGATIVE)
    row_top = jnp.max(scores, axis=2)
    weights = jnp.where(usable[None, None, :], jnp.exp(scores - row_top[:, :, None]), 0.0)
    totals = jnp.sum(weights, axis=2)
    mixture = jnp.einsum(
        "qhk,khd->qhd",
        weights.astype(jnp.bfloat16),
        value_block,
        preferred_element_type=jnp.float32,
    )
    return (mixture, row_top, totals)


def combine(earlier, latter):
    row_top = jnp.maximum(earlier[1], latter[1])
    early_scale = jnp.exp(earlier[1] - row_top)
    late_scale = jnp.exp(latter[1] - row_top)
    mixture = earlier[0] * early_scale[:, :, None] + latter[0] * late_scale[:, :, None]
    return (mixture, row_top, earlier[2] * early_scale + latter[2] * late_scale)


def body(new_q, new_k, new_v, cache_k, cache_v, q_gain, k_gain, cache_len, home_blocks):
    row_count, feature_count = new_q.shape
    heads_here = feature_count // HD
    slot_rows = cache_k.shape[0]
    widened_q = new_q.astype(jnp.float32)
    widened_k = new_k.astype(jnp.float32)
    q_square, k_square = lax.psum(
        (jnp.sum(widened_q * widened_q, axis=1), jnp.sum(widened_k * widened_k, axis=1)), "tensor"
    )
    full_width = HEADS * HD
    q_normed = (widened_q * lax.rsqrt(q_square / full_width + 1e-06)[:, None] * q_gain).astype(
        jnp.bfloat16
    )
    k_normed = (widened_k * lax.rsqrt(k_square / full_width + 1e-06)[:, None] * k_gain).astype(
        jnp.bfloat16
    )
    own_queries = q_normed.reshape(row_count, heads_here, HD)
    own_index = lax.axis_index("group")
    partner = jnp.bitwise_xor(own_index, 1)
    blocks = (cache_len + CB - 1) // CB
    own_length = cache_len[own_index]
    home_count = home_blocks[own_index]
    partner_home = home_blocks[partner]
    positions = jnp.arange(slot_rows, dtype=jnp.int32)
    slot_index = positions // CB
    within = positions % CB
    own_keys_cached = cache_k.reshape(slot_rows, heads_here, HD)
    own_values_cached = cache_v.reshape(slot_rows, heads_here, HD)
    own_usable = (slot_index < home_count) & (positions < own_length)
    far_keys, far_values = swapped((cache_k, cache_v), "group", 0)
    block_index = slot_index - partner_home + home_count
    far_usable = (
        (slot_index >= partner_home)
        & (block_index < blocks[own_index])
        & (block_index * CB + within < own_length)
    )
    near_part = partial_block(own_queries, own_keys_cached, own_values_cached, own_usable)
    far_part = partial_block(
        own_queries,
        far_keys.reshape(slot_rows, heads_here, HD),
        far_values.reshape(slot_rows, heads_here, HD),
        far_usable,
    )
    gathered = combine(near_part, far_part)
    own_keys = k_normed.reshape(row_count, heads_here, HD)
    own_values = new_v.reshape(row_count, heads_here, HD)
    mixture, row_top, totals = combine(
        gathered,
        partial_block(own_queries, own_keys, own_values, jnp.ones((row_count,), jnp.bool_)),
    )
    return (mixture / totals[:, :, None]).astype(jnp.bfloat16).reshape(row_count, feature_count)


def solution(mesh):
    placed = (
        P("group", "tensor"),
        P("group", "tensor"),
        P("group", "tensor"),
        P("group", "tensor"),
        P("group", "tensor"),
        P("tensor"),
        P("tensor"),
        P(),
        P(),
    )
    return jax.shard_map(
        body, mesh=mesh, in_specs=placed, out_specs=P("group", "tensor"), check_vma=False
    )
```

profile of v0, /device:TPU:0, one launch (start us, length us, event | category | flops | bytes accessed | tf_op | source)
XLA Modules:
  0.0 190.0 jit_solution(11308659741138057839)
XLA Ops:
  0.0 0.0 copy-start.3
  0.0 7.4 %copy.21 = bf16[896,2560]{0,1:T(8,128)(2,1)} copy(bf16[896,2560]{1,0:T(8,128)(2,1)} %param.12) | data formatting | bytes 9175040 | tf_op args[3]
  7.4 0.5 collective-permute-start
  7.8 0.1 collective-permute-start.1
  7.9 0.0 copy-done.3
  7.9 2.6 %copy.32 = bf16[512,2560]{0,1:T(8,128)(2,1)} copy(bf16[512,2560]{1,0:T(8,128)(2,1)S(1)} %copy-done.3) | data formatting | bytes 5242880 | tf_op args[2]
  10.5 0.0 copy-start.7
  10.5 0.0 copy-start.4
  10.5 3.0 %copy.29 = bf16[512,2560]{0,1:T(8,128)(2,1)S(1)} copy(bf16[512,2560]{1,0:T(8,128)(2,1)} %param.10) | data formatting | bytes 5242880 | tf_op args[1]
  13.5 0.0 copy-start.1
  13.5 1.5 copy-done.1
  15.0 0.0 copy-start.5
  15.0 0.6 fusion.26
  15.6 3.0 %copy.20 = bf16[512,2560]{0,1:T(8,128)(2,1)S(1)} copy(bf16[512,2560]{1,0:T(8,128)(2,1)} %param.9) | data formatting | bytes 5242880 | tf_op args[0]
  18.6 0.0 copy-start
  18.6 0.6 fusion.23
  19.3 0.0 copy-done.7
  19.3 0.7 dynamic_slice.13
  20.0 0.6 dynamic_slice.15
  20.6 6.0 %all-reduce = (f32[512]{0:T(512)S(1)}, f32[512]{0:T(512)S(1)}) all-reduce(f32[512]{0:T(512)S(1)} %fusion.26, f32[512]{0:T(512)S(1)} %fusion.23), channel_id=1, replica_groups=mesh['group'=16,'tensor'=2] {'tensor'}, use_global_device_ids=true, to_apply=%region_5.6 | all-reduce | flops 1024 | bytes 8192 | tf_op jit(solution)/shard_map/psum | solution.py:51
  26.6 0.0 copy-done.4
  26.6 2.4 %fusion.28 = bf16[512,2560]{0,1:T(8,128)(2,1)S(1)} fusion(bf16[512,2560]{0,1:T(8,128)(2,1)} %copy-done.1, f32[2560]{0:T(1024)S(1)} %copy-done.4, f32[512]{0:T(512)S(1)} %get-tuple-element.20), kind=kLoop, calls=%fused_computation.37 | loop fusion | flops 5242880 | bytes 5255168 | tf_op jit(solution)/shard_map/convert_element_type | solution.py:58
  29.0 0.0 copy-done
  29.0 0.0 copy-done.5
  29.0 2.4 %fusion.25 = bf16[512,2560]{0,1:T(8,128)(2,1)S(1)} fusion(bf16[512,2560]{0,1:T(8,128)(2,1)} %copy-done, f32[2560]{0:T(1024)S(1)} %copy-done.5, f32[512]{0:T(512)S(1)} %get-tuple-element.21), kind=kLoop, calls=%fused_computation.34 | loop fusion | flops 5242880 | bytes 5255168 | tf_op jit(solution)/shard_map/convert_element_type | solution.py:55
  31.4 0.0 copy-start.6
  31.4 8.6 %bitcast_reduce_fusion.2 = (f32[512,20]{0,1:T(8,128)S(1)}, f32[20,512,512]{2,1,0:T(8,128)}) fusion(bf16[512,20,128]{0,2,1:T(8,128)(2,1)S(1)} %bitcast.82, bf16[512,20,128]{0,2,1:T(8,128)(2,1)S(1)} %bitcast.77), kind=kOutput, calls=%fused_computation.15 | convolution fusion | flops 1352652800 | bytes 26255360 | tf_op jit(solution)/shard_map/qhd,khd->qhk/dot_general | solution.py:21
  40.0 0.0 copy-done.6
  40.0 0.7 fusion.65
  40.7 2.6 %fusion.54 = (pred[896]{0:T(1024)(128)(4,1)S(1)}, pred[896]{0:T(1024)(128)(4,1)S(1)}) fusion(s32[]{:T(128)} %bitcast.8, s32[]{:T(128)} %bitcast.7, s32[]{:T(128)} %bitcast.1, s32[]{:T(128)} %bitcast), kind=kLoop, calls=%fused_computation.74 | loop fusion | flops 21504 | bytes 1808 | tf_op jit(solution)/shard_map/and | solution.py:77
  43.3 17.6 %bitcast_reduce_fusion.1 = (f32[512,20]{0,1:T(8,128)S(1)}, f32[20,512,896]{2,1,0:T(8,128)}) fusion(pred[896]{0:T(1024)(128)(4,1)S(1)} %get-tuple-element.23, bf16[512,20,128]{0,2,1:T(8,128)(2,1)S(1)} %bitcast.78, bf16[896,20,128]{0,2,1:T(8,128)(2,1)} %bitcast.80), kind=kOutput, calls=%fused_computation.5 | convolution fusion | flops 2376325120 | bytes 43950976 | tf_op jit(solution)/shard_map/qhd,khd->qhk/dot_general | solution.py:21
  60.8 0.0 copy-start.2
  60.8 17.3 %fusion.4 = f32[512,20]{0,1:T(8,128)S(1)} fusion(f32[20,512,896]{2,1,0:T(8,128)} %get-tuple-element.17, f32[512,20]{0,1:T(8,128)S(1)} %get-tuple-element.16, pred[896]{0:T(1024)(128)(4,1)S(1)} %get-tuple-element.23), kind=kLoop, calls=%fused_computation.10 | loop fusion | flops 45864960 | bytes 36782976 | tf_op jit(solution)/shard_map/reduce_sum | solution.py:27
  78.1 0.0 copy-done.2
  78.1 13.2 %fusion.19 = f32[20,512,128]{1,2,0:T(8,128)} fusion(bf16[512,20,128]{0,2,1:T(8,128)(2,1)S(1)} %bitcast.81, f32[20,512,512]{2,1,0:T(8,128)} %get-tuple-element.15, f32[512,20]{0,1:T(8,128)S(1)} %get-tuple-element.14), kind=kOutput, calls=%fused_computation.25 | convolution fusion | flops 1357905920 | bytes 28876800 | tf_op jit(solution)/shard_map/qhk,khd->qhd/dot_general | solution.py:28
  91.4 9.0 %fusion.17 = f32[512,20]{0,1:T(8,128)S(1)} fusion(f32[20,512,512]{2,1,0:T(8,128)} %get-tuple-element.15, f32[512,20]{0,1:T(8,128)S(1)} %get-tuple-element.14), kind=kLoop, calls=%fused_computation.23 | loop fusion | flops 15718400 | bytes 21053440 | tf_op jit(solution)/shard_map/reduce_sum | solution.py:27
  100.3 7.2 %copy.24 = bf16[896,2560]{0,1:T(8,128)(2,1)} copy(bf16[896,2560]{1,0:T(8,128)(2,1)} %param.13) | data formatting | bytes 9175040 | tf_op args[4]
  107.6 18.4 %fusion.11 = f32[20,512,128]{1,2,0:T(8,128)} fusion(bf16[896,20,128]{0,2,1:T(8,128)(2,1)} %bitcast.84, f32[20,512,896]{2,1,0:T(8,128)} %get-tuple-element.17, f32[512,20]{0,1:T(8,128)S(1)} %get-tuple-element.16, pred[896]{0:T(1024)(128)(4,1)S(1)} %get-tuple-element.23), kind=kOutput, calls=%fused_computation.18 | convolution fusion | flops 2394685440 | bytes 46572416 | tf_op jit(solution)/shard_map/qhk,khd->qhd/dot_general | solution.py:28
  126.0 0.0 collective-permute-done
  126.0 17.6 %bitcast_reduce_fusion = (f32[512,20]{0,1:T(8,128)S(1)}, f32[20,512,896]{2,1,0:T(8,128)}) fusion(pred[896]{0:T(1024)(128)(4,1)S(1)} %get-tuple-element.22, bf16[512,20,128]{0,2,1:T(8,128)(2,1)S(1)} %bitcast.79, bf16[896,20,128]{0,2,1:T(8,128)(2,1)} %bitcast.9), kind=kOutput, calls=%fused_computation.1 | convolution fusion | flops 2376325120 | bytes 43950976 | tf_op jit(solution)/shard_map/qhd,khd->qhk/dot_general | solution.py:21
  143.6 17.1 %fusion.6 = f32[512,20]{0,1:T(8,128)S(1)} fusion(f32[20,512,896]{2,1,0:T(8,128)} %get-tuple-element.19, f32[512,20]{0,1:T(8,128)S(1)} %get-tuple-element.18, pred[896]{0:T(1024)(128)(4,1)S(1)} %get-tuple-element.22), kind=kLoop, calls=%fused_computation.12 | loop fusion | flops 45864960 | bytes 36782976 | tf_op jit(solution)/shard_map/reduce_sum | solution.py:27
  160.8 0.0 collective-permute-done.1
  160.8 7.2 %copy.28 = bf16[896,2560]{0,1:T(8,128)(2,1)} copy(bf16[896,2560]{1,0:T(8,128)(2,1)} %collective-permute-done.1) | data formatting | bytes 9175040 | tf_op jit(solution)/shard_map/ppermute | solution.py:17
  168.0 19.2 %fusion.31 = bf16[512,20,128]{0,2,1:T(8,128)(2,1)S(1)} fusion(f32[20,512,128]{1,2,0:T(8,128)} %fusion.19, f32[20,512,128]{1,2,0:T(8,128)} %fusion.11, f32[512,20]{0,1:T(8,128)S(1)} %get-tuple-element.7, f32[512,20]{0,1:T(8,128)S(1)} %get-tuple-element.11, f32[512,20]{0,1:T(8,128)S(1)} %get-tuple-element.10, f32[512,20]{0,1:T(8,128)S(1)} %get-tuple-element.9, ...), kind=kOutput, calls=%fused_computation.41 | convolution fusion | flops 2405171200 | bytes 54641536 | tf_op jit(solution)/shard_map/qhk,khd->qhd/dot_general | solution.py:28
  187.2 2.8 %copy.34 = bf16[512,2560]{1,0:T(8,128)(2,1)} copy(bf16[512,2560]{0,1:T(8,128)(2,1)S(1)} %bitcast.85) | data formatting | bytes 5242880 | tf_op jit(solution)/shard_map/reshape | solution.py:95
  (3 shorter events, 0.1 us)
Async XLA Ops:
  0.0 7.9 %copy-start.3 = (bf16[512,2560]{1,0:T(8,128)(2,1)S(1)}, bf16[512,2560]{1,0:T(8,128)(2,1)}, u32[]{:S(2)}) copy-start(bf16[512,2560]{1,0:T(8,128)(2,1)} %param.11) | copy-start | bytes 7864324
  7.4 118.6 %collective-permute-start = (bf16[896,2560]{0,1:T(8,128)(2,1)}, bf16[896,2560]{0,1:T(8,128)(2,1)}, u32[]{:S(2)}, u32[]{:S(2)}) collective-permute-start(bf16[896,2560]{0,1:T(8,128)(2,1)} %copy.21), channel_id=1, source_target_pairs={{0,2},{2,0},{4,6},{6,4},{8,10},{10,8},{12,14},{14,12},{16,18},{18,... | collective-permute-start | bytes 13762568 | tf_op jit(solution)/shard_map/ppermute | solution.py:17
  7.8 152.9 %collective-permute-start.1 = (bf16[896,2560]{1,0:T(8,128)(2,1)}, bf16[896,2560]{1,0:T(8,128)(2,1)}, u32[]{:S(2)}, u32[]{:S(2)}) collective-permute-start(bf16[896,2560]{1,0:T(8,128)(2,1)} %param.13), channel_id=1, source_target_pairs={{0,2},{2,0},{4,6},{6,4},{8,10},{10,8},{12,14},{14,12},{16,18},{18,... | collective-permute-start | bytes 13762568 | tf_op jit(solution)/shard_map/ppermute | solution.py:17
  10.5 8.8 %copy-start.7 = (s32[16]{0:T(128)S(1)}, s32[16]{0:T(128)}, u32[]{:S(2)}) copy-start(s32[16]{0:T(128)} %param.16) | copy-start | bytes 196
  10.5 16.1 %copy-start.4 = (f32[2560]{0:T(1024)S(1)}, f32[2560]{0:T(1024)}, u32[]{:S(2)}) copy-start(f32[2560]{0:T(1024)} %param.15) | copy-start | bytes 30724
  13.5 1.5 copy-start.1
  15.0 14.0 %copy-start.5 = (f32[2560]{0:T(1024)S(1)}, f32[2560]{0:T(1024)}, u32[]{:S(2)}) copy-start(f32[2560]{0:T(1024)} %param.14) | copy-start | bytes 30724
  18.6 10.4 %copy-start = (bf16[512,2560]{0,1:T(8,128)(2,1)}, bf16[512,2560]{0,1:T(8,128)(2,1)S(1)}, u32[]{:S(2)}) copy-start(bf16[512,2560]{0,1:T(8,128)(2,1)S(1)} %copy.20) | copy-start | bytes 7864324
  31.4 8.6 %copy-start.6 = (s32[16]{0:T(128)S(1)}, s32[16]{0:T(128)}, u32[]{:S(2)}) copy-start(s32[16]{0:T(128)} %param.17) | copy-start | bytes 196
  60.8 17.3 %copy-start.2 = (bf16[512,2560]{0,1:T(8,128)(2,1)S(1)}, bf16[512,2560]{0,1:T(8,128)(2,1)}, u32[]{:S(2)}) copy-start(bf16[512,2560]{0,1:T(8,128)(2,1)} %copy.32) | copy-start | bytes 7864324
where the time goes:
time: 191 us; the launch traced here: 190 us
  matrix products  94.5 us (49%)
  other arithmetic  52.1 us (27%)
  local copies, waits for them, and re-layouts  36.7 us (19%)
  blocking collectives  6 us (3%)
    dot_general x3, matrix products, partial_block(): jnp.einsum('qhk,khd->qhd', weights.astype(jnp.bfloat16), value_block, pre...  50.8 us
    dot_general x3, matrix products, partial_block(): jnp.einsum('qhd,khd->qhk', queries, key_block, preferred_element_type=jnp...  43.7 us
    reduce_sum x3, other arithmetic, partial_block(): totals = jnp.sum(weights, axis=2)  43.4 us
    unnamed x21, local copies, waits for them, and re-layouts  24.7 us
    ppermute x1, local copies, waits for them, and re-layouts, swapped(): return lax.ppermute(value, axis, pairs)  7.25 us
    psum x1, blocking collectives, body(): lax.psum((jnp.sum(widened_q * widened_q, axis=1), jnp.sum(widened_k * wid...  6 us
  transfers between devices with their start and end apart: 2, of which 0 were waited for; matrix products, arithmetic and copies ran while one was open for 76% of the time, Pallas kernels for 0%

commit v1 on v0

v1 whole, which is shorter than its diff:
```python
import functools
import math

import jax
import jax.numpy as jnp
from jax import lax
from jax.experimental import pallas as pl
from jax.experimental.pallas import tpu as pltpu
from jax.sharding import PartitionSpec as P

HEADS = 40
HD = 128
CB = 128
EPS = 1e-06
NEGATIVE = -1e30
SCALE = math.log2(math.e) / math.sqrt(HD)
SUM_LANE = 64
VMEM = 40 * 1024 * 1024


def swap_pairs(count):
    return [(source, source ^ 1) for source in range(count)]


def row_scale(square, width, factor):
    scale = lax.rsqrt(square / width + EPS) * factor
    pieces = []
    for start in range(0, square.shape[1], HD):
        piece = jnp.broadcast_to(scale[:, start : start + HD], (HD, HD))
        pieces.append(jnp.transpose(piece))
    return jnp.concatenate(pieces, axis=0)


def counts(me_ref, len_ref, home_ref, slots):
    me = me_ref[0]
    partner = jnp.bitwise_xor(me, 1)
    own_home = jnp.clip(home_ref[me], 1, slots)
    far_home = jnp.clip(home_ref[partner], 1, slots)
    own_blocks = lax.shift_right_arithmetic(len_ref[me] + (CB - 1), 7)
    far_blocks = lax.shift_right_arithmetic(len_ref[partner] + (CB - 1), 7)
    own_tail = jnp.minimum(len_ref[me] - (own_home - 1) * CB, CB)
    far_tail = len_ref[partner] - (far_blocks - 1) * CB
    held = jnp.clip(far_blocks - far_home, 0, slots - own_home)
    away = jnp.clip(own_blocks - own_home, 0, slots - far_home)
    return own_home, own_tail, held, far_tail, away


def early_heads(away, heads, slots, fresh):
    result = jnp.int32(0)
    for count in range(1, slots):
        share = min(heads, int(round(count * heads / (slots + fresh))))
        result = jnp.where(away == count, share, result)
    return result


def total_of(refs, row):
    total = refs[0][row : row + 1, :]
    for ref in refs[1:]:
        total = total + ref[row : row + 1, :]
    return total


def lanes(head):
    return pl.ds(pl.multiple_of(head * HD, HD), HD)


class Stage:
    def __init__(self, q, q_scale, q_gain, keys, values, tail, fresh, out, stat, scratch):
        self.q, self.q_scale, self.q_gain = q, q_scale, q_gain
        self.keys, self.values, self.tail, self.fresh = keys, values, tail, fresh
        self.out, self.stat = out, stat
        self.scores, self.tops, self.weights = scratch
        self.rows = q.shape[0] // 2
        self.cached = keys.shape[0]
        self.total = self.cached + (fresh[0].shape[0] if fresh else 0)
        self.lane = lax.broadcasted_iota(jnp.int32, (self.rows, HD), 1)

    def piece(self, half):
        return pl.ds(half * self.rows, self.rows)

    def score(self, head, half):
        cut, piece = lanes(head), self.piece(half)
        raw = self.q[piece, cut].astype(jnp.float32)
        queries = (raw * self.q_scale[piece, :] * self.q_gain[:, cut]).astype(jnp.bfloat16)
        keys = self.keys[:, cut]
        if self.fresh:
            new_k, _, k_scale, k_gain = self.fresh
            raw_k = new_k[:, cut].astype(jnp.float32)
            keys = jnp.concatenate([keys, (raw_k * k_scale[...] * k_gain[:, cut]).astype(jnp.bfloat16)], axis=0)
        scores = lax.dot_general(queries, keys, (((1,), (1,)), ((), ())), preferred_element_type=jnp.float32)
        top = None
        for start in range(0, self.total, CB):
            column = scores[:, start : start + CB]
            if start == self.cached - CB:
                column = jnp.where(self.lane < self.tail, column, NEGATIVE)
            self.scores[half][:, start : start + CB] = column
            top = column if top is None else jnp.maximum(top, column)
        top = jnp.broadcast_to(jnp.max(top, axis=1, keepdims=True), (self.rows, HD))
        self.tops[half][...] = top

    def soften(self, head, half):
        top = self.tops[half][...]
        for start in range(0, self.total, CB):
            column = self.scores[half][:, start : start + CB]
            self.weights[half][:, start : start + CB] = jnp.exp2(column - top).astype(jnp.bfloat16)
        pltpu.store(self.stat.at[self.piece(half), :], top, mask=self.lane == head)

    def mix(self, head, slot, lane, half):
        cut = lanes(head)
        values = self.values[:, cut]
        if self.fresh:
            values = jnp.concatenate([values, self.fresh[1][:, cut]], axis=0)
        wide = jnp.concatenate([values, jnp.ones_like(values)], axis=1)
        mixture = jnp.dot(self.weights[half][:, : self.total], wide, preferred_element_type=jnp.float32)
        totals = mixture[:, HD:]
        inverse = pl.reciprocal(totals, approx=True)
        inverse = inverse * (2.0 - totals * inverse)
        self.out[self.piece(half), lanes(slot)] = (mixture[:, :HD] * inverse).astype(jnp.bfloat16)
        pltpu.store(self.stat.at[self.piece(half), :], totals, mask=self.lane == lane + SUM_LANE)

    def run(self, first, last, spare, ready, done):
        ready(first, True)
        self.score(first, 0)

        def step(head, carry):
            later = jnp.minimum(head + 1, last - 1)
            begun = head > first
            before = jnp.maximum(head - 1, first)
            ready(head + 1, False)
            self.score(head, 1)
            self.soften(head, 0)
            self.mix(before, jnp.where(begun, before, spare), jnp.where(begun, before, SUM_LANE - 1), 1)
            self.score(later, 0)
            self.soften(head, 1)
            self.mix(head, head, head, 0)

            @pl.when(begun)
            def _():
                done(before).start()

            return carry

        lax.fori_loop(first, last, step, 0)
        self.mix(last - 1, last - 1, last - 1, 1)
        done(last - 1).start()
        lax.fori_loop(first, last, lambda head, carry: (done(head).wait(), carry)[1], 0)


def loads(arrays, chunk, heads, sems):
    width = chunk * HD

    def copies(part):
        cut = pl.ds(pl.multiple_of(part * width, width), width)
        result = []
        for index, (source, target, rows) in enumerate(arrays):
            left = source.at[:, cut] if rows is None else source.at[rows, cut]
            right = target.at[:, cut] if rows is None else target.at[pl.ds(0, rows.size), cut]
            result.append(pltpu.make_async_copy(left, right, sems.at[index, part]))
        return result

    def start(first, last):
        def one(part, carry):
            for copy in copies(part):
                copy.start()
            return carry

        lax.fori_loop(first // chunk, (last + chunk - 1) // chunk, one, 0)

    def ready(first, last):
        def wait(head, at_start):
            if at_start:
                wanted = True
            else:
                wanted = (head < last) & (lax.rem(head, chunk) == 0)

            @pl.when(wanted)
            def _():
                for copy in copies(head // chunk):
                    copy.wait()

        return wait

    return start, ready


def early_kernel(me_ref, len_ref, home_ref, *refs, slots, heads, chunk, sums):
    own_squares, far_squares, refs = refs[:sums], refs[sums : 2 * sums], refs[2 * sums :]
    (q_any, far_q_any, k_any, v_any, nk_any, nv_any, qg, kg, far_any, far_stat_any, own_any, stat_any) = refs[:12]
    q, k, v, nk, nv, out, stat, q_scale, k_scale, s0, s1, t0, t1, w0, w1, in_sems, out_sems, stat_sem = refs[12:]
    own_home, own_tail, held, far_tail, away = counts(me_ref, len_ref, home_ref, slots)
    fresh_rows = nk.shape[0]
    scratch = ((s0, s1), (t0, t1), (w0, w1))

    def writer(target):
        def copy(head):
            return pltpu.make_async_copy(out.at[:, lanes(head)], target.at[:, lanes(head)], out_sems.at[head])

        return copy

    def write_stat(target):
        copy = pltpu.make_async_copy(stat, target, stat_sem)
        copy.start()
        copy.wait()

    for count in range(1, slots):

        @pl.when(held == count)
        def _():
            size = count * CB
            rows = pl.ds(pl.multiple_of(jnp.minimum(own_home, slots - count) * CB, CB), size)
            start, ready = loads([(far_q_any, q, None), (k_any, k, rows), (v_any, v, rows)], chunk, heads, in_sems)
            start(0, heads)
            q_scale[...] = row_scale(total_of(far_squares, 0), HEADS * HD, SCALE)
            Stage(
                q, q_scale, qg, k.at[pl.ds(0, size), :], v.at[pl.ds(0, size), :], far_tail, None, out, stat, scratch
            ).run(0, heads, heads, ready(0, heads), writer(far_any))
            write_stat(far_stat_any)

    last = early_heads(away, heads, slots, fresh_rows // CB)

    @pl.when(last > 0)
    def _():
        start, ready = loads(
            [(q_any, q, None), (k_any, k, None), (v_any, v, None), (nk_any, nk, None), (nv_any, nv, None)],
            chunk, heads, in_sems,
        )
        start(0, last)
        q_scale[...] = row_scale(total_of(own_squares, 0), HEADS * HD, SCALE)
        k_scale[...] = row_scale(total_of(own_squares, 1), HEADS * HD, 1.0)
        Stage(q, q_scale, qg, k, v, own_tail, (nk, nv, k_scale, kg), out, stat, scratch).run(
            0, last, heads, ready(0, last), writer(own_any)
        )
        write_stat(stat_any)


def late_kernel(me_ref, len_ref, home_ref, *refs, slots, heads, chunk, sums):
    own_squares, refs = refs[:sums], refs[sums:]
    (q_any, k_any, v_any, nk_any, nv_any, qg, kg, _, _, own_any, stat_any) = refs[:11]
    q, k, v, nk, nv, out, stat, q_scale, k_scale, s0, s1, t0, t1, w0, w1, in_sems, out_sems, stat_sem = refs[11:]
    own_home, own_tail, held, far_tail, away = counts(me_ref, len_ref, home_ref, slots)
    fresh_rows = nk.shape[0]
    scratch = ((s0, s1), (t0, t1), (w0, w1))
    first = early_heads(away, heads, slots, fresh_rows // CB)

    def writer(head):
        return pltpu.make_async_copy(out.at[:, lanes(head)], own_any.at[:, lanes(head)], out_sems.at[head])

    for count in range(1, slots + 1):

        @pl.when((own_home == count) & (first < heads))
        def _():
            rows = pl.ds(0, count * CB)
            start, ready = loads(
                [(q_any, q, None), (k_any, k, rows), (v_any, v, rows), (nk_any, nk, None), (nv_any, nv, None)],
                chunk, heads, in_sems,
            )
            start(first, heads)

            @pl.when(first > 0)
            def _():
                copy = pltpu.make_async_copy(stat_any, stat, stat_sem)
                copy.start()
                copy.wait()

            q_scale[...] = row_scale(total_of(own_squares, 0), HEADS * HD, SCALE)
            k_scale[...] = row_scale(total_of(own_squares, 1), HEADS * HD, 1.0)
            Stage(
                q, q_scale, qg, k.at[rows, :], v.at[rows, :], own_tail, (nk, nv, k_scale, kg), out, stat, scratch
            ).run(first, heads, heads, ready(first, heads), writer)

            @pl.when(away > 0)
            def _():
                copy = pltpu.make_async_copy(stat, stat_any, stat_sem)
                copy.start()
                copy.wait()


def join_kernel(
    me_ref, len_ref, home_ref, own_any, stat_any, far_any, far_stat_any, out_any,
    own, far, stat, far_stat, in_sems, out_sems, *, slots, step_rows
):
    away = counts(me_ref, len_ref, home_ref, slots)[4]
    row_count = own.shape[0]
    steps = row_count // step_rows

    @pl.when(away > 0)
    def _():
        def piece(step):
            return pl.ds(pl.multiple_of(step * step_rows, step_rows), step_rows)

        def copies(step):
            rows = piece(step)
            pairs = ((own_any, own), (far_any, far), (stat_any, stat), (far_stat_any, far_stat))
            return [
                pltpu.make_async_copy(a.at[rows, :], b.at[rows, :], in_sems.at[i, step]) for i, (a, b) in enumerate(pairs)
            ]

        def write(step):
            return pltpu.make_async_copy(own.at[piece(step), :], out_any.at[piece(step), :], out_sems.at[step])

        for step in range(steps):
            for copy in copies(step):
                copy.start()

        def one(step, carry):
            for copy in copies(step):
                copy.wait()
            rows = piece(step)
            near, away_stat = stat[rows, :], far_stat[rows, :]
            top = jnp.maximum(near, away_stat)
            own_part = pltpu.roll(near, HD - SUM_LANE, 1) * jnp.exp2(near - top)
            far_part = pltpu.roll(away_stat, HD - SUM_LANE, 1) * jnp.exp2(away_stat - top)
            share = far_part / (own_part + far_part)
            for head in range(own.shape[1] // HD):
                cut = slice(head * HD, (head + 1) * HD)
                here = own[rows, cut].astype(jnp.float32)
                there = far[rows, cut].astype(jnp.float32)
                own[rows, cut] = (here + share[:, head : head + 1] * (there - here)).astype(jnp.bfloat16)
            write(step).start()
            return carry

        lax.fori_loop(0, steps, one, 0)
        for step in range(steps):
            write(step).wait()


def body(groups, tensors, new_q, new_k, new_v, cache_k, cache_v, q_gain, k_gain, cache_len, home_blocks):
    row_count, feature_count = new_q.shape
    heads = feature_count // HD
    slot_rows = cache_k.shape[0]
    slots = slot_rows // CB
    chunk = 2 if heads % 2 == 0 else 1
    half, keys = row_count // 2, slot_rows + row_count

    far_q = lax.ppermute(new_q, "group", swap_pairs(groups))
    wide_q = new_q.astype(jnp.float32)
    wide_k = new_k.astype(jnp.float32)
    squares = jnp.stack([jnp.sum(wide_q * wide_q, axis=1), jnp.sum(wide_k * wide_k, axis=1)])
    if tensors == 2:
        diagonal = [(source, source ^ 3) for source in range(groups * tensors)]
        own_squares = [squares, lax.ppermute(squares, "tensor", swap_pairs(tensors))]
        far_squares = [
            lax.ppermute(squares, "group", swap_pairs(groups)),
            lax.ppermute(squares, ("group", "tensor"), diagonal),
        ]
    else:
        own_squares = [lax.psum(squares, "tensor")]
        far_squares = [lax.ppermute(own_squares[0], "group", swap_pairs(groups))]
    sums = len(own_squares)

    me = lax.axis_index("group").astype(jnp.int32).reshape(1)
    q_gain = q_gain.reshape(1, feature_count)
    k_gain = k_gain.reshape(1, feature_count)
    scalars = (me, cache_len, home_blocks)
    smem = [pl.BlockSpec(memory_space=pltpu.SMEM)] * 3
    vmem = pl.BlockSpec(memory_space=pltpu.VMEM)
    anywhere = pl.BlockSpec(memory_space=pl.ANY)

    stat = jax.ShapeDtypeStruct((row_count, HD), jnp.float32)
    result = jax.ShapeDtypeStruct((row_count, feature_count), jnp.bfloat16)
    new_rows = pltpu.VMEM((row_count, feature_count), jnp.bfloat16)
    slot_space = pltpu.VMEM((slot_rows, feature_count), jnp.bfloat16)
    stat_space = pltpu.VMEM((row_count, HD), jnp.float32)
    space = [
        new_rows, slot_space, slot_space, new_rows, new_rows,
        pltpu.VMEM((row_count, feature_count + HD), jnp.bfloat16),
        stat_space, stat_space, stat_space,
        pltpu.VMEM((half, keys), jnp.float32), pltpu.VMEM((half, keys), jnp.float32),
        pltpu.VMEM((half, HD), jnp.float32), pltpu.VMEM((half, HD), jnp.float32),
        pltpu.VMEM((half, keys), jnp.bfloat16), pltpu.VMEM((half, keys), jnp.bfloat16),
        pltpu.SemaphoreType.DMA((5, heads // chunk)), pltpu.SemaphoreType.DMA((heads,)), pltpu.SemaphoreType.DMA,
    ]
    pairs = row_count * heads * CB

    def cost(blocks):
        return pl.CostEstimate(
            flops=4 * pairs * HD * blocks, bytes_accessed=4 * blocks * CB * feature_count, transcendentals=pairs * blocks
        )

    def params(size):
        return pltpu.CompilerParams(vmem_limit_bytes=size)

    far_out, far_stat, own_out, own_stat = pl.pallas_call(
        functools.partial(early_kernel, slots=slots, heads=heads, chunk=chunk, sums=sums),
        out_shape=(result, stat, result, stat),
        in_specs=smem + [vmem] * (2 * sums) + [anywhere] * 6 + [vmem] * 2,
        out_specs=(anywhere,) * 4,
        scratch_shapes=space,
        compiler_params=params(VMEM),
        cost_estimate=cost(6),
        name="early_attention",
    )(*scalars, *own_squares, *far_squares, new_q, far_q, cache_k, cache_v, new_k, new_v, q_gain, k_gain)
    back_out, back_stat = lax.ppermute((far_out, far_stat), "group", swap_pairs(groups))

    own_out, own_stat = pl.pallas_call(
        functools.partial(late_kernel, slots=slots, heads=heads, chunk=chunk, sums=sums),
        out_shape=(result, stat),
        in_specs=smem + [vmem] * sums + [anywhere] * 5 + [vmem] * 2 + [anywhere] * 2,
        out_specs=(anywhere,) * 2,
        scratch_shapes=space,
        input_output_aliases={10 + sums: 0, 11 + sums: 1},
        compiler_params=params(VMEM),
        cost_estimate=cost(6),
        name="late_attention",
    )(*scalars, *own_squares, new_q, cache_k, cache_v, new_k, new_v, q_gain, k_gain, own_out, own_stat)

    step_rows = 64
    steps = row_count // step_rows
    return pl.pallas_call(
        functools.partial(join_kernel, slots=slots, step_rows=step_rows),
        out_shape=result,
        in_specs=smem + [anywhere] * 4,
        out_specs=anywhere,
        scratch_shapes=[
            new_rows, new_rows, stat_space, stat_space,
            pltpu.SemaphoreType.DMA((4, steps)), pltpu.SemaphoreType.DMA((steps,)),
        ],
        input_output_aliases={3: 0},
        compiler_params=params(16 * 1024 * 1024),
        name="join_parts",
    )(*scalars, own_out, own_stat, back_out, back_stat)


def solution(mesh):
    placed = (
        P("group", "tensor"),
        P("group", "tensor"),
        P("group", "tensor"),
        P("group", "tensor"),
        P("group", "tensor"),
        P("tensor"),
        P("tensor"),
        P(),
        P(),
    )
    return jax.shard_map(
        functools.partial(body, mesh.shape["group"], mesh.shape["tensor"]),
        mesh=mesh,
        in_specs=placed,
        out_specs=P("group", "tensor"),
        check_vma=False,
    )
```

time: 191 us -> 54.8 us (0.29)
  the two profiles are of different devices: /device:TPU:0 before, /device:TPU:21 now
where the time goes in v1:
time: 54.8 us; the launch traced here: 55.2 us
  Pallas kernels  36.7 us (67%)
  starting transfers between devices  7.26 us (13%)
  local copies, waits for them, and re-layouts  5.82 us (11%)
  other arithmetic  3 us (5%)
  waiting for transfers between devices  2.17 us (4%)
    pallas_call x1, Pallas kernels, body(): pl.pallas_call(functools.partial(late_kernel, slots=slots, heads=heads, c...  24.2 us
    pallas_call x1, Pallas kernels, body(): pl.pallas_call(functools.partial(early_kernel, slots=slots, heads=heads,...  6.39 us
    pallas_call x1, Pallas kernels, body(): pl.pallas_call(functools.partial(join_kernel, slots=slots, step_rows=step...  6.05 us
    unnamed x20, local copies, waits for them, and re-layouts  5.8 us
    ppermute x2, starting transfers between devices, body(): lax.ppermute((far_out, far_stat), 'group', swap_pairs(groups))  4.58 us
    reduce_sum x1, other arithmetic, body(): jnp.sum(wide_q * wide_q, axis=1)  2.41 us
    ppermute x1, starting transfers between devices, body(): lax.ppermute(squares, ('group', 'tensor'), diagonal)  1.25 us
    ppermute x1, waiting for transfers between devices, body(): lax.ppermute(squares, ('group', 'tensor'), diagonal)  1.13 us
  transfers between devices with their start and end apart: 6, of which 2 were waited for; matrix products, arithmetic and copies ran while one was open for 5% of the time, Pallas kernels for 44%

profile of v1, /device:TPU:21, one launch (start us, length us, event | category | flops | bytes accessed | tf_op | source)
XLA Modules:
  0.0 55.2 jit_solution(3569555546532349902)
XLA Ops:
  0.0 0.0 copy-start
  0.0 0.0 copy-start.8
  0.0 0.0 copy-start.9
  0.0 0.0 copy-start.7
  0.0 0.0 copy-start.6
  0.0 0.7 %collective-permute-start.3 = (bf16[512,2560]{1,0:T(8,128)(2,1)}, bf16[512,2560]{1,0:T(8,128)(2,1)}, u32[]{:S(2)}, u32[]{:S(2)}) collective-permute-start(bf16[512,2560]{1,0:T(8,128)(2,1)} %refs_2_.1), channel_id=1, source_target_pairs={{0,2},{2,0},{4,6},{6,4},{8,10},{10,8},{12,14},{14,12},{16,18},{18,... | collective-permute-start | bytes 7864328 | tf_op jit(solution)/shard_map/ppermute | solution.py:335
  0.8 2.4 %multiply_reduce_fusion.1 = f32[512]{0:T(512)S(1)} fusion(bf16[512,2560]{1,0:T(8,128)(2,1)} %refs_2_.1), kind=kLoop, calls=%fused_computation.1 | loop fusion | flops 3931648 | bytes 2623488 | tf_op jit(solution)/shard_map/reduce_sum | solution.py:338
  3.2 0.0 copy-done
  3.2 0.6 %multiply_reduce_fusion = f32[512]{0:T(512)S(1)} fusion(bf16[512,2560]{1,0:T(8,128)(2,1)S(1)} %copy-done), kind=kLoop, calls=%fused_computation | loop fusion | flops 3931648 | bytes 2623488 | tf_op jit(solution)/shard_map/reduce_sum | solution.py:338
  3.8 1.2 %collective-permute-start.2 = (f32[2,512]{1,0:T(2,128)S(1)}, f32[2,512]{1,0:T(2,128)S(1)}, u32[]{:S(2)}, u32[]{:S(2)}) collective-permute-start(f32[2,512]{1,0:T(2,128)S(1)} %pad_maximum_fusion.refs_0_), channel_id=1, source_target_pairs={{0,3},{1,2},{2,1},{3,0},{4,7},{5,6},{6,5},{7,4},{8,11},{9,10},{10,... | collective-permute-start | bytes 12296 | tf_op jit(solution)/shard_map/ppermute | solution.py:344
  5.0 0.4 collective-permute-start.1
  5.5 0.3 collective-permute-start
  5.7 0.0 copy-done.8
  5.7 0.0 copy-done.9
  5.8 1.1 %collective-permute-done.2.refs_3_ = f32[2,512]{1,0:T(2,128)S(1)} collective-permute-done((f32[2,512]{1,0:T(2,128)S(1)}, f32[2,512]{1,0:T(2,128)S(1)}, u32[]{:S(2)}, u32[]{:S(2)}) %collective-permute-start.2) | collective-permute-done | bytes 4128 | tf_op jit(solution)/shard_map/ppermute | solution.py:344
  6.9 0.0 collective-permute-done.1.refs_2_
  6.9 1.0 %collective-permute-done.refs_1_ = f32[2,512]{1,0:T(2,128)S(1)} collective-permute-done((f32[2,512]{1,0:T(2,128)S(1)}, f32[2,512]{1,0:T(2,128)S(1)}, u32[]{:S(2)}, u32[]{:S(2)}) %collective-permute-start) | collective-permute-done | bytes 4128 | tf_op jit(solution)/shard_map/ppermute | solution.py:341
  7.9 0.0 collective-permute-done.3.refs_5_
  7.9 0.0 copy-done.7
  7.9 0.0 copy-done.6
  7.9 0.0 copy-start.1
  7.9 1.7 %copy-done.1 = bf16[512,2560]{1,0:T(8,128)(2,1)S(1)} copy-done((bf16[512,2560]{1,0:T(8,128)(2,1)S(1)}, bf16[512,2560]{1,0:T(8,128)(2,1)}, u32[]{:S(2)}) %copy-start.1) | copy-done | bytes 2621464
  9.7 0.0 copy-start.4
  9.7 1.7 %copy-done.4 = bf16[512,2560]{1,0:T(8,128)(2,1)S(1)} copy-done((bf16[512,2560]{1,0:T(8,128)(2,1)S(1)}, bf16[512,2560]{1,0:T(8,128)(2,1)}, u32[]{:S(2)}) %copy-start.4) | copy-done | bytes 2621464
  11.4 0.0 copy-start.2
  11.4 0.0 copy-start.5
  11.4 6.4 %early_attention.1 = (bf16[512,2560]{1,0:T(8,128)(2,1)S(1)}, f32[512,128]{1,0:T(8,128)S(1)}, bf16[512,2560]{1,0:T(8,128)(2,1)}, f32[512,128]{1,0:T(8,128)S(1)}) custom-call(s32[1]{0:T(128)} %bitcast.me_ref, s32[16]{0:T(128)S(1)} %copy-done.6, s32[16]{0:T(128)S(1)} %copy-done.7, f32[2,512]{1,0:T(2,128)S(1)} %pad_maximum_fusion.refs_0_, ...), custom_call_target="tpu_custom_call" | custom-call | flops 4026531840 | bytes 7864320 | tf_op jit(solution)/shard_map/early_attention/pallas_call | solution.py:383
  17.8 4.5 %collective-permute-start.4 = (bf16[512,2560]{1,0:T(8,128)(2,1)S(1)}, bf16[512,2560]{1,0:T(8,128)(2,1)S(1)}, u32[]{:S(2)}, u32[]{:S(2)}) collective-permute-start(bf16[512,2560]{1,0:T(8,128)(2,1)S(1)} %get-tuple-element.15), channel_id=1, source_target_pairs={{0,2},{2,0},{4,6},{6,4},{8,10},{10,8},{12,14},{14,12},{16,18},{18,... | collective-permute-start | bytes 7864328 | tf_op jit(solution)/shard_map/ppermute | solution.py:393
  22.3 0.1 collective-permute-start.5
  22.4 0.0 copy-done.2
  22.4 0.0 copy-done.5
  22.4 0.0 copy-start.3
  22.4 2.3 %copy-done.3 = bf16[896,2560]{1,0:T(8,128)(2,1)S(1)} copy-done((bf16[896,2560]{1,0:T(8,128)(2,1)S(1)}, bf16[896,2560]{1,0:T(8,128)(2,1)}, u32[]{:S(2)}) %copy-start.3) | copy-done | bytes 4587544
  24.7 24.2 %late_attention.1 = (bf16[512,2560]{1,0:T(8,128)(2,1)}, f32[512,128]{1,0:T(8,128)S(1)}) custom-call(s32[1]{0:T(128)} %bitcast.me_ref, s32[16]{0:T(128)S(1)} %copy-done.6, s32[16]{0:T(128)S(1)} %copy-done.7, f32[2,512]{1,0:T(2,128)S(1)} %pad_maximum_fusion.refs_0_, ...), custom_call_target="tpu_custom_call", output_to_operand_aliasing={{0}: (12, {}), {1}: (13, {})} | custom-call | flops 4026531840 | bytes 7864320 | tf_op jit(solution)/shard_map/late_attention/pallas_call | solution.py:395
  48.9 0.0 collective-permute-done.5.far_stat_any
  48.9 0.0 collective-permute-done.4.far_any
  49.0 6.0 %join_parts.1 = bf16[512,2560]{1,0:T(8,128)(2,1)} custom-call(s32[1]{0:T(128)} %bitcast.me_ref, s32[16]{0:T(128)S(1)} %copy-done.6, s32[16]{0:T(128)S(1)} %copy-done.7, bf16[512,2560]{1,0:T(8,128)(2,1)} %get-tuple-element.13.own_any, f32[512,128]{1,0:T(8,128)S(1)} %get-tuple-element.14.stat_any, ...), custom_call_target="tpu_custom_call", output_to_operand_aliasing={{}: (3, {})} | custom-call | tf_op jit(solution)/shard_map/join_parts/pallas_call | solution.py:409
  (3 shorter events, 0.0 us)
Async XLA Ops:
  0.0 3.2 %copy-start = (bf16[512,2560]{1,0:T(8,128)(2,1)S(1)}, bf16[512,2560]{1,0:T(8,128)(2,1)}, u32[]{:S(2)}) copy-start(bf16[512,2560]{1,0:T(8,128)(2,1)} %refs_5_.1) | copy-start | bytes 7864324
  0.0 5.7 %copy-start.8 = (f32[2560]{0:T(1024)S(1)}, f32[2560]{0:T(1024)}, u32[]{:S(2)}) copy-start(f32[2560]{0:T(1024)} %param.14) | copy-start | bytes 30724
  0.0 5.7 %copy-start.9 = (f32[2560]{0:T(1024)S(1)}, f32[2560]{0:T(1024)}, u32[]{:S(2)}) copy-start(f32[2560]{0:T(1024)} %param.15) | copy-start | bytes 30724
  0.0 7.9 %copy-start.7 = (s32[16]{0:T(128)S(1)}, s32[16]{0:T(128)}, u32[]{:S(2)}) copy-start(s32[16]{0:T(128)} %home_ref.5) | copy-start | bytes 196
  0.0 7.9 %copy-start.6 = (s32[16]{0:T(128)S(1)}, s32[16]{0:T(128)}, u32[]{:S(2)}) copy-start(s32[16]{0:T(128)} %len_ref.5) | copy-start | bytes 196
  0.0 7.9 %collective-permute-start.3 = (bf16[512,2560]{1,0:T(8,128)(2,1)}, bf16[512,2560]{1,0:T(8,128)(2,1)}, u32[]{:S(2)}, u32[]{:S(2)}) collective-permute-start(bf16[512,2560]{1,0:T(8,128)(2,1)} %refs_2_.1), channel_id=1, source_target_pairs={{0,2},{2,0},{4,6},{6,4},{8,10},{10,8},{12,14},{14,12},{16,18},{18,... | collective-permute-start | bytes 7864328 | tf_op jit(solution)/shard_map/ppermute | solution.py:335
  3.8 3.1 %collective-permute-start.2 = (f32[2,512]{1,0:T(2,128)S(1)}, f32[2,512]{1,0:T(2,128)S(1)}, u32[]{:S(2)}, u32[]{:S(2)}) collective-permute-start(f32[2,512]{1,0:T(2,128)S(1)} %pad_maximum_fusion.refs_0_), channel_id=1, source_target_pairs={{0,3},{1,2},{2,1},{3,0},{4,7},{5,6},{6,5},{7,4},{8,11},{9,10},{10,... | collective-permute-start | bytes 12296 | tf_op jit(solution)/shard_map/ppermute | solution.py:344
  5.0 1.9 %collective-permute-start.1 = (f32[2,512]{1,0:T(2,128)S(1)}, f32[2,512]{1,0:T(2,128)S(1)}, u32[]{:S(2)}, u32[]{:S(2)}) collective-permute-start(f32[2,512]{1,0:T(2,128)S(1)} %pad_maximum_fusion.refs_0_), channel_id=1, source_target_pairs={{0,2},{2,0},{4,6},{6,4},{8,10},{10,8},{12,14},{14,12},{16,18},{18,... | collective-permute-start | bytes 12296 | tf_op jit(solution)/shard_map/ppermute | solution.py:343
  5.5 2.5 %collective-permute-start = (f32[2,512]{1,0:T(2,128)S(1)}, f32[2,512]{1,0:T(2,128)S(1)}, u32[]{:S(2)}, u32[]{:S(2)}) collective-permute-start(f32[2,512]{1,0:T(2,128)S(1)} %pad_maximum_fusion.refs_0_), channel_id=1, source_target_pairs={{0,1},{1,0},{2,3},{3,2},{4,5},{5,4},{6,7},{7,6},{8,9},{9,8},{10,11... | collective-permute-start | bytes 12296 | tf_op jit(solution)/shard_map/ppermute | solution.py:341
  7.9 1.7 %copy-start.1 = (bf16[512,2560]{1,0:T(8,128)(2,1)S(1)}, bf16[512,2560]{1,0:T(8,128)(2,1)}, u32[]{:S(2)}) copy-start(bf16[512,2560]{1,0:T(8,128)(2,1)} %refs_2_.1) | copy-start | bytes 7864324
  9.7 1.7 %copy-start.4 = (bf16[512,2560]{1,0:T(8,128)(2,1)S(1)}, bf16[512,2560]{1,0:T(8,128)(2,1)}, u32[]{:S(2)}) copy-start(bf16[512,2560]{1,0:T(8,128)(2,1)} %refs_6_.3) | copy-start | bytes 7864324
  11.4 11.0 %copy-start.2 = (bf16[512,2560]{1,0:T(8,128)(2,1)S(1)}, bf16[512,2560]{1,0:T(8,128)(2,1)}, u32[]{:S(2)}) copy-start(bf16[512,2560]{1,0:T(8,128)(2,1)} %refs_2_.1) | copy-start | bytes 7864324
  11.4 11.0 %copy-start.5 = (bf16[512,2560]{1,0:T(8,128)(2,1)S(1)}, bf16[512,2560]{1,0:T(8,128)(2,1)}, u32[]{:S(2)}) copy-start(bf16[512,2560]{1,0:T(8,128)(2,1)} %refs_6_.3) | copy-start | bytes 7864324
  17.8 31.1 %collective-permute-start.4 = (bf16[512,2560]{1,0:T(8,128)(2,1)S(1)}, bf16[512,2560]{1,0:T(8,128)(2,1)S(1)}, u32[]{:S(2)}, u32[]{:S(2)}) collective-permute-start(bf16[512,2560]{1,0:T(8,128)(2,1)S(1)} %get-tuple-element.15), channel_id=1, source_target_pairs={{0,2},{2,0},{4,6},{6,4},{8,10},{10,8},{12,14},{14,12},{16,18},{18,... | collective-permute-start | bytes 7864328 | tf_op jit(solution)/shard_map/ppermute | solution.py:393
  22.3 26.6 %collective-permute-start.5 = (f32[512,128]{1,0:T(8,128)S(1)}, f32[512,128]{1,0:T(8,128)S(1)}, u32[]{:S(2)}, u32[]{:S(2)}) collective-permute-start(f32[512,128]{1,0:T(8,128)S(1)} %get-tuple-element.16), channel_id=1, source_target_pairs={{0,2},{2,0},{4,6},{6,4},{8,10},{10,8},{12,14},{14,12},{16,18},{18,... | collective-permute-start | bytes 786440 | tf_op jit(solution)/shard_map/ppermute | solution.py:393
  22.4 2.3 %copy-start.3 = (bf16[896,2560]{1,0:T(8,128)(2,1)S(1)}, bf16[896,2560]{1,0:T(8,128)(2,1)}, u32[]{:S(2)}) copy-start(bf16[896,2560]{1,0:T(8,128)(2,1)} %refs_3_.1) | copy-start | bytes 13762564

commit v2 on v1

--- a/solution.py
+++ b/solution.py
@@ -15,7 +15,8 @@
 NEGATIVE = -1e30
 SCALE = math.log2(math.e) / math.sqrt(HD)
 SUM_LANE = 64
-VMEM = 40 * 1024 * 1024
+VMEM = 48 * 1024 * 1024
+KEYS = 256
 
 
 def swap_pairs(count):
@@ -48,7 +49,7 @@
 def early_heads(away, heads, slots, fresh):
     result = jnp.int32(0)
     for count in range(1, slots):
-        share = min(heads, int(round(count * heads / (slots + fresh))))
+        share = min(heads, 2 * int(round(count * heads / (slots + fresh) / 2)))
         result = jnp.where(away == count, share, result)
     return result
 
@@ -70,69 +71,74 @@
         self.keys, self.values, self.tail, self.fresh = keys, values, tail, fresh
         self.out, self.stat = out, stat
         self.scores, self.tops, self.weights = scratch
-        self.rows = q.shape[0] // 2
+        self.rows = q.shape[0]
         self.cached = keys.shape[0]
         self.total = self.cached + (fresh[0].shape[0] if fresh else 0)
         self.lane = lax.broadcasted_iota(jnp.int32, (self.rows, HD), 1)
 
-    def piece(self, half):
-        return pl.ds(half * self.rows, self.rows)
-
-    def score(self, head, half):
-        cut, piece = lanes(head), self.piece(half)
-        raw = self.q[piece, cut].astype(jnp.float32)
-        queries = (raw * self.q_scale[piece, :] * self.q_gain[:, cut]).astype(jnp.bfloat16)
+    def score(self, head, slot):
+        cut = lanes(head)
+        raw = self.q[:, cut].astype(jnp.float32)
+        queries = (raw * self.q_scale[...] * self.q_gain[:, cut]).astype(jnp.bfloat16)
         keys = self.keys[:, cut]
         if self.fresh:
             new_k, _, k_scale, k_gain = self.fresh
             raw_k = new_k[:, cut].astype(jnp.float32)
             keys = jnp.concatenate([keys, (raw_k * k_scale[...] * k_gain[:, cut]).astype(jnp.bfloat16)], axis=0)
-        scores = lax.dot_general(queries, keys, (((1,), (1,)), ((), ())), preferred_element_type=jnp.float32)
         top = None
+        for begin in range(0, self.total, KEYS):
+            scores = lax.dot_general(
+                queries, keys[begin : begin + KEYS], (((1,), (1,)), ((), ())), preferred_element_type=jnp.float32
+            )
+            for start in range(begin, min(begin + KEYS, self.total), CB):
+                column = scores[:, start - begin : start - begin + CB]
+                if start == self.cached - CB:
+                    column = jnp.where(self.lane < self.tail, column, NEGATIVE)
+                self.scores[slot][:, start : start + CB] = column
+                top = column if top is None else jnp.maximum(top, column)
+        self.tops[slot][...] = jnp.broadcast_to(jnp.max(top, axis=1, keepdims=True), (self.rows, HD))
+
+    def soften(self, head, slot):
+        top = self.tops[slot][...]
         for start in range(0, self.total, CB):
-            column = scores[:, start : start + CB]
-            if start == self.cached - CB:
-                column = jnp.where(self.lane < self.tail, column, NEGATIVE)
-            self.scores[half][:, start : start + CB] = column
-            top = column if top is None else jnp.maximum(top, column)
-        top = jnp.broadcast_to(jnp.max(top, axis=1, keepdims=True), (self.rows, HD))
-        self.tops[half][...] = top
-
-    def soften(self, head, half):
-        top = self.tops[half][...]
-        for start in range(0, self.total, CB):
-            column = self.scores[half][:, start : start + CB]
-            self.weights[half][:, start : start + CB] = jnp.exp2(column - top).astype(jnp.bfloat16)
-        pltpu.store(self.stat.at[self.piece(half), :], top, mask=self.lane == head)
-
-    def mix(self, head, slot, lane, half):
+            column = self.scores[slot][:, start : start + CB]
+            self.weights[slot][:, start : start + CB] = jnp.exp2(column - top).astype(jnp.bfloat16)
+        pltpu.store(self.stat, top, mask=self.lane == head)
+
+    def mix(self, head, target, lane, slot):
         cut = lanes(head)
         values = self.values[:, cut]
         if self.fresh:
             values = jnp.concatenate([values, self.fresh[1][:, cut]], axis=0)
         wide = jnp.concatenate([values, jnp.ones_like(values)], axis=1)
-        mixture = jnp.dot(self.weights[half][:, : self.total], wide, preferred_element_type=jnp.float32)
+        mixture = jnp.dot(self.weights[slot][:, : self.total], wide, preferred_element_type=jnp.float32)
         totals = mixture[:, HD:]
         inverse = pl.reciprocal(totals, approx=True)
         inverse = inverse * (2.0 - totals * inverse)
-        self.out[self.piece(half), lanes(slot)] = (mixture[:, :HD] * inverse).astype(jnp.bfloat16)
-        pltpu.store(self.stat.at[self.piece(half), :], totals, mask=self.lane == lane + SUM_LANE)
-
-    def run(self, first, last, spare, ready, done):
+        self.out[:, lanes(target)] = (mixture[:, :HD] * inverse).astype(jnp.bfloat16)
+        pltpu.store(self.stat, totals, mask=self.lane == lane + SUM_LANE)
+
+    def run(self, first, last, spare, ready, done, finish=None):
         ready(first, True)
         self.score(first, 0)
-
-        def step(head, carry):
-            later = jnp.minimum(head + 1, last - 1)
-            begun = head > first
+        count = last - first
+        paired = lax.rem(count, 2) == 0
+
+        def step(index, carry):
+            head = first + 2 * index
+            second = jnp.minimum(head + 1, last - 1)
+            later = jnp.minimum(head + 2, last - 1)
+            begun = index > 0
             before = jnp.maximum(head - 1, first)
             ready(head + 1, False)
-            self.score(head, 1)
+            ready(head + 2, False)
+            self.score(second, 1)
             self.soften(head, 0)
             self.mix(before, jnp.where(begun, before, spare), jnp.where(begun, before, SUM_LANE - 1), 1)
             self.score(later, 0)
-            self.soften(head, 1)
+            self.soften(second, 1)
             self.mix(head, head, head, 0)
+            done(head).start()
 
             @pl.when(begun)
             def _():
@@ -140,9 +146,15 @@
 
             return carry
 
-        lax.fori_loop(first, last, step, 0)
-        self.mix(last - 1, last - 1, last - 1, 1)
-        done(last - 1).start()
+        lax.fori_loop(0, lax.shift_right_logical(count + 1, 1), step, 0)
+        self.mix(last - 1, jnp.where(paired, last - 1, spare), last - 1, 1)
+
+        @pl.when(paired)
+        def _():
+            done(last - 1).start()
+
+        if finish is not None:
+            finish()
         lax.fori_loop(first, last, lambda head, carry: (done(head).wait(), carry)[1], 0)
 
 
@@ -158,13 +170,15 @@
             result.append(pltpu.make_async_copy(left, right, sems.at[index, part]))
         return result
 
-    def start(first, last):
+    def start(first, last, between):
         def one(part, carry):
             for copy in copies(part):
                 copy.start()
             return carry
 
-        lax.fori_loop(first // chunk, (last + chunk - 1) // chunk, one, 0)
+        one(first // chunk, 0)
+        between()
+        lax.fori_loop(first // chunk + 1, (last + chunk - 1) // chunk, one, 0)
 
     def ready(first, last):
         def wait(head, at_start):
@@ -198,9 +212,14 @@
         return copy
 
     def write_stat(target):
-        copy = pltpu.make_async_copy(stat, target, stat_sem)
-        copy.start()
-        copy.wait()
+        return pltpu.make_async_copy(stat, target, stat_sem)
+
+    def far_scale():
+        q_scale[...] = row_scale(total_of(far_squares, 0), HEADS * HD, SCALE)
+
+    def own_scale():
+        q_scale[...] = row_scale(total_of(own_squares, 0), HEADS * HD, SCALE)
+        k_scale[...] = row_scale(total_of(own_squares, 1), HEADS * HD, 1.0)
 
     for count in range(1, slots):
 
@@ -209,12 +228,11 @@
             size = count * CB
             rows = pl.ds(pl.multiple_of(jnp.minimum(own_home, slots - count) * CB, CB), size)
             start, ready = loads([(far_q_any, q, None), (k_any, k, rows), (v_any, v, rows)], chunk, heads, in_sems)
-            start(0, heads)
-            q_scale[...] = row_scale(total_of(far_squares, 0), HEADS * HD, SCALE)
+            start(0, heads, far_scale)
             Stage(
                 q, q_scale, qg, k.at[pl.ds(0, size), :], v.at[pl.ds(0, size), :], far_tail, None, out, stat, scratch
-            ).run(0, heads, heads, ready(0, heads), writer(far_any))
-            write_stat(far_stat_any)
+            ).run(0, heads, heads, ready(0, heads), writer(far_any), write_stat(far_stat_any).start)
+            write_stat(far_stat_any).wait()
 
     last = early_heads(away, heads, slots, fresh_rows // CB)
 
@@ -224,13 +242,11 @@
             [(q_any, q, None), (k_any, k, None), (v_any, v, None), (nk_any, nk, None), (nv_any, nv, None)],
             chunk, heads, in_sems,
         )
-        start(0, last)
-        q_scale[...] = row_scale(total_of(own_squares, 0), HEADS * HD, SCALE)
-        k_scale[...] = row_scale(total_of(own_squares, 1), HEADS * HD, 1.0)
+        start(0, last, own_scale)
         Stage(q, q_scale, qg, k, v, own_tail, (nk, nv, k_scale, kg), out, stat, scratch).run(
-            0, last, heads, ready(0, last), writer(own_any)
+            0, last, heads, ready(0, last), writer(own_any), write_stat(stat_any).start
         )
-        write_stat(stat_any)
+        write_stat(stat_any).wait()
 
 
 def late_kernel(me_ref, len_ref, home_ref, *refs, slots, heads, chunk, sums):
@@ -242,6 +258,10 @@
     scratch = ((s0, s1), (t0, t1), (w0, w1))
     first = early_heads(away, heads, slots, fresh_rows // CB)
 
+    def own_scale():
+        q_scale[...] = row_scale(total_of(own_squares, 0), HEADS * HD, SCALE)
+        k_scale[...] = row_scale(total_of(own_squares, 1), HEADS * HD, 1.0)
+
     def writer(head):
         return pltpu.make_async_copy(out.at[:, lanes(head)], own_any.at[:, lanes(head)], out_sems.at[head])
 
@@ -254,7 +274,7 @@
                 [(q_any, q, None), (k_any, k, rows), (v_any, v, rows), (nk_any, nk, None), (nv_any, nv, None)],
                 chunk, heads, in_sems,
             )
-            start(first, heads)
+            start(first, heads, own_scale)
 
             @pl.when(first > 0)
             def _():
@@ -262,8 +282,6 @@
                 copy.start()
                 copy.wait()
 
-            q_scale[...] = row_scale(total_of(own_squares, 0), HEADS * HD, SCALE)
-            k_scale[...] = row_scale(total_of(own_squares, 1), HEADS * HD, 1.0)
             Stage(
                 q, q_scale, qg, k.at[rows, :], v.at[rows, :], own_tail, (nk, nv, k_scale, kg), out, stat, scratch
             ).run(first, heads, heads, ready(first, heads), writer)
@@ -282,6 +300,7 @@
     away = counts(me_ref, len_ref, home_ref, slots)[4]
     row_count = own.shape[0]
     steps = row_count // step_rows
+    width = 2 * HD if own.shape[1] % (2 * HD) == 0 else HD
 
     @pl.when(away > 0)
     def _():
@@ -310,12 +329,19 @@
             top = jnp.maximum(near, away_stat)
             own_part = pltpu.roll(near, HD - SUM_LANE, 1) * jnp.exp2(near - top)
             far_part = pltpu.roll(away_stat, HD - SUM_LANE, 1) * jnp.exp2(away_stat - top)
-            share = far_part / (own_part + far_part)
-            for head in range(own.shape[1] // HD):
-                cut = slice(head * HD, (head + 1) * HD)
+            known = lax.broadcasted_iota(jnp.int32, near.shape, 1) < own.shape[1] // HD
+            share = jnp.where(known, far_part / (own_part + far_part), 0.0)
+            high = share.astype(jnp.bfloat16)
+            for begin in range(0, own.shape[1], width):
+                cut = slice(begin, begin + width)
+                lane = lax.broadcasted_iota(jnp.int32, (HD, width), 0)
+                column = lax.broadcasted_iota(jnp.int32, (HD, width), 1)
+                first = (lane - begin // HD) * HD
+                spread = ((column >= first) & (column < first + HD)).astype(jnp.bfloat16)
+                wide = jnp.dot(high, spread, preferred_element_type=jnp.float32)
                 here = own[rows, cut].astype(jnp.float32)
                 there = far[rows, cut].astype(jnp.float32)
-                own[rows, cut] = (here + share[:, head : head + 1] * (there - here)).astype(jnp.bfloat16)
+                own[rows, cut] = (here + wide * (there - here)).astype(jnp.bfloat16)
             write(step).start()
             return carry
 
@@ -329,23 +355,19 @@
     heads = feature_count // HD
     slot_rows = cache_k.shape[0]
     slots = slot_rows // CB
-    chunk = 2 if heads % 2 == 0 else 1
-    half, keys = row_count // 2, slot_rows + row_count
+    chunk = 4 if heads % 4 == 0 else 1
+    half, keys = row_count, slot_rows + row_count
 
     far_q = lax.ppermute(new_q, "group", swap_pairs(groups))
     wide_q = new_q.astype(jnp.float32)
     wide_k = new_k.astype(jnp.float32)
     squares = jnp.stack([jnp.sum(wide_q * wide_q, axis=1), jnp.sum(wide_k * wide_k, axis=1)])
     if tensors == 2:
-        diagonal = [(source, source ^ 3) for source in range(groups * tensors)]
-        own_squares = [squares, lax.ppermute(squares, "tensor", swap_pairs(tensors))]
-        far_squares = [
-            lax.ppermute(squares, "group", swap_pairs(groups)),
-            lax.ppermute(squares, ("group", "tensor"), diagonal),
-        ]
+        squares = squares + lax.ppermute(squares, "tensor", swap_pairs(tensors))
     else:
-        own_squares = [lax.psum(squares, "tensor")]
-        far_squares = [lax.ppermute(own_squares[0], "group", swap_pairs(groups))]
+        squares = lax.psum(squares, "tensor")
+    own_squares = [squares]
+    far_squares = [lax.ppermute(squares, "group", swap_pairs(groups))]
     sums = len(own_squares)
 
     me = lax.axis_index("group").astype(jnp.int32).reshape(1)
@@ -355,6 +377,7 @@
     smem = [pl.BlockSpec(memory_space=pltpu.SMEM)] * 3
     vmem = pl.BlockSpec(memory_space=pltpu.VMEM)
     anywhere = pl.BlockSpec(memory_space=pl.ANY)
+    distant = pl.BlockSpec(memory_space=pltpu.HBM)
 
     stat = jax.ShapeDtypeStruct((row_count, HD), jnp.float32)
     result = jax.ShapeDtypeStruct((row_count, feature_count), jnp.bfloat16)
@@ -383,7 +406,7 @@
     far_out, far_stat, own_out, own_stat = pl.pallas_call(
         functools.partial(early_kernel, slots=slots, heads=heads, chunk=chunk, sums=sums),
         out_shape=(result, stat, result, stat),
-        in_specs=smem + [vmem] * (2 * sums) + [anywhere] * 6 + [vmem] * 2,
+        in_specs=smem + [vmem] * (2 * sums) + [distant, anywhere] + [distant] * 4 + [vmem] * 2,
         out_specs=(anywhere,) * 4,
         scratch_shapes=space,
         compiler_params=params(VMEM),
@@ -395,7 +418,7 @@
     own_out, own_stat = pl.pallas_call(
         functools.partial(late_kernel, slots=slots, heads=heads, chunk=chunk, sums=sums),
         out_shape=(result, stat),
-        in_specs=smem + [vmem] * sums + [anywhere] * 5 + [vmem] * 2 + [anywhere] * 2,
+        in_specs=smem + [vmem] * sums + [distant] * 5 + [vmem] * 2 + [anywhere] * 2,
         out_specs=(anywhere,) * 2,
         scratch_shapes=space,
         input_output_aliases={10 + sums: 0, 11 + sums: 1},
@@ -404,7 +427,7 @@
         name="late_attention",
     )(*scalars, *own_squares, new_q, cache_k, cache_v, new_k, new_v, q_gain, k_gain, own_out, own_stat)
 
-    step_rows = 64
+    step_rows = 128
     steps = row_count // step_rows
     return pl.pallas_call(
         functools.partial(join_kernel, slots=slots, step_rows=step_rows),

time: 54.8 us -> 48.7 us (0.89)
  the two profiles are of different devices: /device:TPU:21 before, /device:TPU:4 now
where the time goes in v2:
time: 48.7 us; the launch traced here: 48 us
  Pallas kernels  35.8 us (74%)
  starting transfers between devices  3.75 us (8%)
  waiting for transfers between devices  3.22 us (7%)
  other arithmetic  3.08 us (6%)
  local copies, waits for them, and re-layouts  1.78 us (4%)
    pallas_call x1, Pallas kernels, body(): pl.pallas_call(functools.partial(late_kernel, slots=slots, heads=heads, c...  23.4 us
    pallas_call x1, Pallas kernels, body(): pl.pallas_call(functools.partial(early_kernel, slots=slots, heads=heads,...  6.82 us
    pallas_call x1, Pallas kernels, body(): pl.pallas_call(functools.partial(join_kernel, slots=slots, step_rows=step...  5.59 us
    reduce_sum x1, other arithmetic, body(): jnp.sum(wide_q * wide_q, axis=1)  2.48 us
    ppermute x1, waiting for transfers between devices, body(): squares = squares + lax.ppermute(squares, 'tensor', swap_pairs(tensors))  2.12 us
    ppermute x2, starting transfers between devices, body(): lax.ppermute((far_out, far_stat), 'group', swap_pairs(groups))  2.05 us
    unnamed x14, local copies, waits for them, and re-layouts  1.76 us
    ppermute x1, starting transfers between devices, body(): squares = squares + lax.ppermute(squares, 'tensor', swap_pairs(tensors))  1.56 us
  transfers between devices with their start and end apart: 5, of which 2 were waited for; matrix products, arithmetic and copies ran while one was open for 6% of the time, Pallas kernels for 49%

profile of v2, /device:TPU:4, one launch (start us, length us, event | category | flops | bytes accessed | tf_op | source)
XLA Modules:
  0.0 48.0 jit_solution(11853792241992421205)
XLA Ops:
  0.0 0.0 copy-start
  0.0 0.0 copy-start.5
  0.0 0.0 copy-start.6
  0.0 0.0 copy-start.4
  0.0 0.0 copy-start.3
  0.0 0.1 collective-permute-start.2
  0.1 2.5 %multiply_reduce_fusion.1 = f32[512]{0:T(512)S(1)} fusion(bf16[512,2560]{1,0:T(8,128)(2,1)} %refs_1_.1), kind=kLoop, calls=%fused_computation.1 | loop fusion | flops 3931648 | bytes 2623488 | tf_op jit(solution)/shard_map/reduce_sum | solution.py:364
  2.6 0.0 copy-done
  2.6 0.6 %multiply_reduce_fusion = f32[512]{0:T(512)S(1)} fusion(bf16[512,2560]{1,0:T(8,128)(2,1)S(1)} %copy-done), kind=kLoop, calls=%fused_computation | loop fusion | flops 3931648 | bytes 2623488 | tf_op jit(solution)/shard_map/reduce_sum | solution.py:364
  3.2 1.6 %collective-permute-start = (f32[2,512]{1,0:T(2,128)S(1)}, f32[2,512]{1,0:T(2,128)S(1)}, u32[]{:S(2)}, u32[]{:S(2)}) collective-permute-start(f32[2,512]{1,0:T(2,128)S(1)} %pad_maximum_fusion), channel_id=1, source_target_pairs={{0,1},{1,0},{2,3},{3,2},{4,5},{5,4},{6,7},{7,6},{8,9},{9,8},{10,11... | collective-permute-start | bytes 12296 | tf_op jit(solution)/shard_map/ppermute | solution.py:366
  4.8 2.1 %collective-permute-done = f32[2,512]{1,0:T(2,128)S(1)} collective-permute-done((f32[2,512]{1,0:T(2,128)S(1)}, f32[2,512]{1,0:T(2,128)S(1)}, u32[]{:S(2)}, u32[]{:S(2)}) %collective-permute-start) | collective-permute-done | bytes 4128 | tf_op jit(solution)/shard_map/ppermute | solution.py:366
  6.9 0.1 collective-permute-start.1
  7.0 0.0 copy-done.5
  7.0 0.0 copy-done.6
  7.0 1.1 %collective-permute-done.1.refs_1_ = f32[2,512]{1,0:T(2,128)S(1)} collective-permute-done((f32[2,512]{1,0:T(2,128)S(1)}, f32[2,512]{1,0:T(2,128)S(1)}, u32[]{:S(2)}, u32[]{:S(2)}) %collective-permute-start.1) | collective-permute-done | bytes 4128 | tf_op jit(solution)/shard_map/ppermute | solution.py:370
  8.1 0.0 collective-permute-done.2.refs_3_
  8.1 0.0 copy-done.4
  8.1 0.0 copy-done.3
  8.1 0.0 copy-start.2
  8.1 1.7 %copy-done.2 = bf16[512,2560]{1,0:T(8,128)(2,1)S(1)} copy-done((bf16[512,2560]{1,0:T(8,128)(2,1)S(1)}, bf16[512,2560]{1,0:T(8,128)(2,1)}, u32[]{:S(2)}) %copy-start.2) | copy-done | bytes 2621464
  9.9 0.0 copy-start.1
  9.9 6.8 %early_attention.1 = (bf16[512,2560]{1,0:T(8,128)(2,1)}, f32[512,128]{1,0:T(8,128)S(1)}, bf16[512,2560]{1,0:T(8,128)(2,1)}, f32[512,128]{1,0:T(8,128)S(1)}) custom-call(s32[1]{0:T(128)} %bitcast.me_ref, s32[16]{0:T(128)S(1)} %copy-done.3, s32[16]{0:T(128)S(1)} %copy-done.4, f32[2,512]{1,0:T(2,128)S(1)} %fusion.refs_0_, ...), custom_call_target="tpu_custom_call" | custom-call | flops 4026531840 | bytes 7864320 | tf_op jit(solution)/shard_map/early_attention/pallas_call | solution.py:406
  16.7 2.0 %collective-permute-start.3 = (bf16[512,2560]{1,0:T(8,128)(2,1)}, bf16[512,2560]{1,0:T(8,128)(2,1)S(1)}, u32[]{:S(2)}, u32[]{:S(2)}) collective-permute-start(bf16[512,2560]{1,0:T(8,128)(2,1)} %get-tuple-element.15), channel_id=1, source_target_pairs={{0,2},{2,0},{4,6},{6,4},{8,10},{10,8},{12,14},{14,12},{16,18},{18,... | collective-permute-start | bytes 7864328 | tf_op jit(solution)/shard_map/ppermute | solution.py:416
  18.7 0.1 collective-permute-start.4
  18.7 0.0 copy-done.1
  18.8 23.4 %late_attention.1 = (bf16[512,2560]{1,0:T(8,128)(2,1)}, f32[512,128]{1,0:T(8,128)S(1)}) custom-call(s32[1]{0:T(128)} %bitcast.me_ref, s32[16]{0:T(128)S(1)} %copy-done.3, s32[16]{0:T(128)S(1)} %copy-done.4, f32[2,512]{1,0:T(2,128)S(1)} %fusion.refs_0_, bf16[512,2560]{1,0:T(8,128)(2,1)S(1)} %copy-done.2, ...), custom_call_target="tpu_custom_call", output_to_operand_aliasing={{0}: (11, {}), {1}: (12, {})} | custom-call | flops 4026531840 | bytes 7864320 | tf_op jit(solution)/shard_map/late_attention/pallas_call | solution.py:418
  42.2 0.0 collective-permute-done.4.far_stat_any
  42.2 0.0 collective-permute-done.3.far_any
  42.2 5.6 %join_parts.1 = bf16[512,2560]{1,0:T(8,128)(2,1)} custom-call(s32[1]{0:T(128)} %bitcast.me_ref, s32[16]{0:T(128)S(1)} %copy-done.3, s32[16]{0:T(128)S(1)} %copy-done.4, bf16[512,2560]{1,0:T(8,128)(2,1)} %get-tuple-element.13.own_any, f32[512,128]{1,0:T(8,128)S(1)} %get-tuple-element.14.stat_any, ...), custom_call_target="tpu_custom_call", output_to_operand_aliasing={{}: (3, {})} | custom-call | tf_op jit(solution)/shard_map/join_parts/pallas_call | solution.py:432
  (4 shorter events, 0.0 us)
Async XLA Ops:
  0.0 2.6 %copy-start = (bf16[512,2560]{1,0:T(8,128)(2,1)S(1)}, bf16[512,2560]{1,0:T(8,128)(2,1)}, u32[]{:S(2)}) copy-start(bf16[512,2560]{1,0:T(8,128)(2,1)} %refs_4_.3) | copy-start | bytes 7864324
  0.0 7.0 %copy-start.5 = (f32[2560]{0:T(1024)S(1)}, f32[2560]{0:T(1024)}, u32[]{:S(2)}) copy-start(f32[2560]{0:T(1024)} %param.14) | copy-start | bytes 30724
  0.0 7.0 %copy-start.6 = (f32[2560]{0:T(1024)S(1)}, f32[2560]{0:T(1024)}, u32[]{:S(2)}) copy-start(f32[2560]{0:T(1024)} %param.15) | copy-start | bytes 30724
  0.0 8.1 %copy-start.4 = (s32[16]{0:T(128)S(1)}, s32[16]{0:T(128)}, u32[]{:S(2)}) copy-start(s32[16]{0:T(128)} %home_ref.5) | copy-start | bytes 196
  0.0 8.1 %copy-start.3 = (s32[16]{0:T(128)S(1)}, s32[16]{0:T(128)}, u32[]{:S(2)}) copy-start(s32[16]{0:T(128)} %len_ref.5) | copy-start | bytes 196
  0.0 8.1 %collective-permute-start.2 = (bf16[512,2560]{1,0:T(8,128)(2,1)}, bf16[512,2560]{1,0:T(8,128)(2,1)}, u32[]{:S(2)}, u32[]{:S(2)}) collective-permute-start(bf16[512,2560]{1,0:T(8,128)(2,1)} %refs_1_.1), channel_id=1, source_target_pairs={{0,2},{2,0},{4,6},{6,4},{8,10},{10,8},{12,14},{14,12},{16,18},{18,... | collective-permute-start | bytes 7864328 | tf_op jit(solution)/shard_map/ppermute | solution.py:361
  3.2 3.7 %collective-permute-start = (f32[2,512]{1,0:T(2,128)S(1)}, f32[2,512]{1,0:T(2,128)S(1)}, u32[]{:S(2)}, u32[]{:S(2)}) collective-permute-start(f32[2,512]{1,0:T(2,128)S(1)} %pad_maximum_fusion), channel_id=1, source_target_pairs={{0,1},{1,0},{2,3},{3,2},{4,5},{5,4},{6,7},{7,6},{8,9},{9,8},{10,11... | collective-permute-start | bytes 12296 | tf_op jit(solution)/shard_map/ppermute | solution.py:366
  6.9 1.2 %collective-permute-start.1 = (f32[2,512]{1,0:T(2,128)S(1)}, f32[2,512]{1,0:T(2,128)S(1)}, u32[]{:S(2)}, u32[]{:S(2)}) collective-permute-start(f32[2,512]{1,0:T(2,128)S(1)} %fusion.refs_0_), channel_id=1, source_target_pairs={{0,2},{2,0},{4,6},{6,4},{8,10},{10,8},{12,14},{14,12},{16,18},{18,... | collective-permute-start | bytes 12296 | tf_op jit(solution)/shard_map/ppermute | solution.py:370
  8.1 1.7 %copy-start.2 = (bf16[512,2560]{1,0:T(8,128)(2,1)S(1)}, bf16[512,2560]{1,0:T(8,128)(2,1)}, u32[]{:S(2)}) copy-start(bf16[512,2560]{1,0:T(8,128)(2,1)} %refs_1_.1) | copy-start | bytes 7864324
  9.9 8.9 %copy-start.1 = (bf16[512,2560]{1,0:T(8,128)(2,1)S(1)}, bf16[512,2560]{1,0:T(8,128)(2,1)}, u32[]{:S(2)}) copy-start(bf16[512,2560]{1,0:T(8,128)(2,1)} %refs_4_.3) | copy-start | bytes 7864324
  16.7 25.5 %collective-permute-start.3 = (bf16[512,2560]{1,0:T(8,128)(2,1)}, bf16[512,2560]{1,0:T(8,128)(2,1)S(1)}, u32[]{:S(2)}, u32[]{:S(2)}) collective-permute-start(bf16[512,2560]{1,0:T(8,128)(2,1)} %get-tuple-element.15), channel_id=1, source_target_pairs={{0,2},{2,0},{4,6},{6,4},{8,10},{10,8},{12,14},{14,12},{16,18},{18,... | collective-permute-start | bytes 7864328 | tf_op jit(solution)/shard_map/ppermute | solution.py:416
  18.7 23.5 %collective-permute-start.4 = (f32[512,128]{1,0:T(8,128)S(1)}, f32[512,128]{1,0:T(8,128)S(1)}, u32[]{:S(2)}, u32[]{:S(2)}) collective-permute-start(f32[512,128]{1,0:T(8,128)S(1)} %get-tuple-element.16), channel_id=1, source_target_pairs={{0,2},{2,0},{4,6},{6,4},{8,10},{10,8},{12,14},{14,12},{16,18},{18,... | collective-permute-start | bytes 786440 | tf_op jit(solution)/shard_map/ppermute | solution.py:416

commit v3 on v2

--- a/solution.py
+++ b/solution.py
@@ -15,7 +15,7 @@
 NEGATIVE = -1e30
 SCALE = math.log2(math.e) / math.sqrt(HD)
 SUM_LANE = 64
-VMEM = 48 * 1024 * 1024
+VMEM = 53 * 1024 * 1024
 KEYS = 256
 
 
@@ -32,15 +32,17 @@
     return jnp.concatenate(pieces, axis=0)
 
 
-def counts(me_ref, len_ref, home_ref, slots):
-    me = me_ref[0]
+def counts(facts_ref, slots):
+    requests = (facts_ref.shape[0] - 1) // 2
+    me = facts_ref[0]
     partner = jnp.bitwise_xor(me, 1)
-    own_home = jnp.clip(home_ref[me], 1, slots)
-    far_home = jnp.clip(home_ref[partner], 1, slots)
-    own_blocks = lax.shift_right_arithmetic(len_ref[me] + (CB - 1), 7)
-    far_blocks = lax.shift_right_arithmetic(len_ref[partner] + (CB - 1), 7)
-    own_tail = jnp.minimum(len_ref[me] - (own_home - 1) * CB, CB)
-    far_tail = len_ref[partner] - (far_blocks - 1) * CB
+    own_length, far_length = facts_ref[1 + me], facts_ref[1 + partner]
+    own_home = jnp.clip(facts_ref[1 + requests + me], 1, slots)
+    far_home = jnp.clip(facts_ref[1 + requests + partner], 1, slots)
+    own_blocks = lax.shift_right_arithmetic(own_length + (CB - 1), 7)
+    far_blocks = lax.shift_right_arithmetic(far_length + (CB - 1), 7)
+    own_tail = jnp.minimum(own_length - (own_home - 1) * CB, CB)
+    far_tail = far_length - (far_blocks - 1) * CB
     held = jnp.clip(far_blocks - far_home, 0, slots - own_home)
     away = jnp.clip(own_blocks - own_home, 0, slots - far_home)
     return own_home, own_tail, held, far_tail, away
@@ -197,11 +199,11 @@
     return start, ready
 
 
-def early_kernel(me_ref, len_ref, home_ref, *refs, slots, heads, chunk, sums):
+def early_kernel(facts_ref, *refs, slots, heads, chunk, sums):
     own_squares, far_squares, refs = refs[:sums], refs[sums : 2 * sums], refs[2 * sums :]
     (q_any, far_q_any, k_any, v_any, nk_any, nv_any, qg, kg, far_any, far_stat_any, own_any, stat_any) = refs[:12]
     q, k, v, nk, nv, out, stat, q_scale, k_scale, s0, s1, t0, t1, w0, w1, in_sems, out_sems, stat_sem = refs[12:]
-    own_home, own_tail, held, far_tail, away = counts(me_ref, len_ref, home_ref, slots)
+    own_home, own_tail, held, far_tail, away = counts(facts_ref, slots)
     fresh_rows = nk.shape[0]
     scratch = ((s0, s1), (t0, t1), (w0, w1))
 
@@ -249,11 +251,11 @@
         write_stat(stat_any).wait()
 
 
-def late_kernel(me_ref, len_ref, home_ref, *refs, slots, heads, chunk, sums):
+def late_kernel(facts_ref, *refs, slots, heads, chunk, sums):
     own_squares, refs = refs[:sums], refs[sums:]
     (q_any, k_any, v_any, nk_any, nv_any, qg, kg, _, _, own_any, stat_any) = refs[:11]
     q, k, v, nk, nv, out, stat, q_scale, k_scale, s0, s1, t0, t1, w0, w1, in_sems, out_sems, stat_sem = refs[11:]
-    own_home, own_tail, held, far_tail, away = counts(me_ref, len_ref, home_ref, slots)
+    own_home, own_tail, held, far_tail, away = counts(facts_ref, slots)
     fresh_rows = nk.shape[0]
     scratch = ((s0, s1), (t0, t1), (w0, w1))
     first = early_heads(away, heads, slots, fresh_rows // CB)
@@ -294,13 +296,12 @@
 
 
 def join_kernel(
-    me_ref, len_ref, home_ref, own_any, stat_any, far_any, far_stat_any, out_any,
-    own, far, stat, far_stat, in_sems, out_sems, *, slots, step_rows
+    facts_ref, own_any, stat_any, far_any, far_stat_any, out_any,
+    own, far, stat, far_stat, spread, out, in_sems, out_sems, *, slots, step_rows
 ):
-    away = counts(me_ref, len_ref, home_ref, slots)[4]
+    away = counts(facts_ref, slots)[4]
     row_count = own.shape[0]
     steps = row_count // step_rows
-    width = 2 * HD if own.shape[1] % (2 * HD) == 0 else HD
 
     @pl.when(away > 0)
     def _():
@@ -315,11 +316,15 @@
             ]
 
         def write(step):
-            return pltpu.make_async_copy(own.at[piece(step), :], out_any.at[piece(step), :], out_sems.at[step])
+            return pltpu.make_async_copy(out.at[piece(step), :], out_any.at[piece(step), :], out_sems.at[step])
 
         for step in range(steps):
             for copy in copies(step):
                 copy.start()
+
+        lane = lax.broadcasted_iota(jnp.int32, spread.shape, 0) * HD
+        column = lax.broadcasted_iota(jnp.int32, spread.shape, 1)
+        spread[...] = ((column >= lane) & (column < lane + HD)).astype(jnp.bfloat16)
 
         def one(step, carry):
             for copy in copies(step):
@@ -331,17 +336,10 @@
             far_part = pltpu.roll(away_stat, HD - SUM_LANE, 1) * jnp.exp2(away_stat - top)
             known = lax.broadcasted_iota(jnp.int32, near.shape, 1) < own.shape[1] // HD
             share = jnp.where(known, far_part / (own_part + far_part), 0.0)
-            high = share.astype(jnp.bfloat16)
-            for begin in range(0, own.shape[1], width):
-                cut = slice(begin, begin + width)
-                lane = lax.broadcasted_iota(jnp.int32, (HD, width), 0)
-                column = lax.broadcasted_iota(jnp.int32, (HD, width), 1)
-                first = (lane - begin // HD) * HD
-                spread = ((column >= first) & (column < first + HD)).astype(jnp.bfloat16)
-                wide = jnp.dot(high, spread, preferred_element_type=jnp.float32)
-                here = own[rows, cut].astype(jnp.float32)
-                there = far[rows, cut].astype(jnp.float32)
-                own[rows, cut] = (here + wide * (there - here)).astype(jnp.bfloat16)
+            wide = jnp.dot(share.astype(jnp.bfloat16), spread[...], preferred_element_type=jnp.float32)
+            here = own[rows, :].astype(jnp.float32)
+            there = far[rows, :].astype(jnp.float32)
+            out[rows, :] = (here + wide * (there - here)).astype(jnp.bfloat16)
             write(step).start()
             return carry
 
@@ -355,7 +353,7 @@
     heads = feature_count // HD
     slot_rows = cache_k.shape[0]
     slots = slot_rows // CB
-    chunk = 4 if heads % 4 == 0 else 1
+    chunk = 2 if heads % 2 == 0 else 1
     half, keys = row_count, slot_rows + row_count
 
     far_q = lax.ppermute(new_q, "group", swap_pairs(groups))
@@ -373,11 +371,10 @@
     me = lax.axis_index("group").astype(jnp.int32).reshape(1)
     q_gain = q_gain.reshape(1, feature_count)
     k_gain = k_gain.reshape(1, feature_count)
-    scalars = (me, cache_len, home_blocks)
-    smem = [pl.BlockSpec(memory_space=pltpu.SMEM)] * 3
+    facts = jnp.concatenate([me, cache_len, home_blocks])
+    smem = [pl.BlockSpec(memory_space=pltpu.SMEM)]
     vmem = pl.BlockSpec(memory_space=pltpu.VMEM)
     anywhere = pl.BlockSpec(memory_space=pl.ANY)
-    distant = pl.BlockSpec(memory_space=pltpu.HBM)
 
     stat = jax.ShapeDtypeStruct((row_count, HD), jnp.float32)
     result = jax.ShapeDtypeStruct((row_count, feature_count), jnp.bfloat16)
@@ -406,28 +403,28 @@
     far_out, far_stat, own_out, own_stat = pl.pallas_call(
         functools.partial(early_kernel, slots=slots, heads=heads, chunk=chunk, sums=sums),
         out_shape=(result, stat, result, stat),
-        in_specs=smem + [vmem] * (2 * sums) + [distant, anywhere] + [distant] * 4 + [vmem] * 2,
+        in_specs=smem + [vmem] * (2 * sums) + [anywhere] * 6 + [vmem] * 2,
         out_specs=(anywhere,) * 4,
         scratch_shapes=space,
         compiler_params=params(VMEM),
         cost_estimate=cost(6),
         name="early_attention",
-    )(*scalars, *own_squares, *far_squares, new_q, far_q, cache_k, cache_v, new_k, new_v, q_gain, k_gain)
+    )(facts, *own_squares, *far_squares, new_q, far_q, cache_k, cache_v, new_k, new_v, q_gain, k_gain)
     back_out, back_stat = lax.ppermute((far_out, far_stat), "group", swap_pairs(groups))
 
     own_out, own_stat = pl.pallas_call(
         functools.partial(late_kernel, slots=slots, heads=heads, chunk=chunk, sums=sums),
         out_shape=(result, stat),
-        in_specs=smem + [vmem] * sums + [distant] * 5 + [vmem] * 2 + [anywhere] * 2,
+        in_specs=smem + [vmem] * sums + [anywhere] * 5 + [vmem] * 2 + [anywhere] * 2,
         out_specs=(anywhere,) * 2,
         scratch_shapes=space,
-        input_output_aliases={10 + sums: 0, 11 + sums: 1},
+        input_output_aliases={8 + sums: 0, 9 + sums: 1},
         compiler_params=params(VMEM),
         cost_estimate=cost(6),
         name="late_attention",
-    )(*scalars, *own_squares, new_q, cache_k, cache_v, new_k, new_v, q_gain, k_gain, own_out, own_stat)
-
-    step_rows = 128
+    )(facts, *own_squares, new_q, cache_k, cache_v, new_k, new_v, q_gain, k_gain, own_out, own_stat)
+
+    step_rows = 64
     steps = row_count // step_rows
     return pl.pallas_call(
         functools.partial(join_kernel, slots=slots, step_rows=step_rows),
@@ -436,12 +433,13 @@
         out_specs=anywhere,
         scratch_shapes=[
             new_rows, new_rows, stat_space, stat_space,
+            pltpu.VMEM((HD, feature_count), jnp.bfloat16), new_rows,
             pltpu.SemaphoreType.DMA((4, steps)), pltpu.SemaphoreType.DMA((steps,)),
         ],
-        input_output_aliases={3: 0},
-        compiler_params=params(16 * 1024 * 1024),
+        input_output_aliases={1: 0},
+        compiler_params=params(24 * 1024 * 1024),
         name="join_parts",
-    )(*scalars, own_out, own_stat, back_out, back_stat)
+    )(facts, own_out, own_stat, back_out, back_stat)
 
 
 def solution(mesh):

time: 48.7 us -> 46.9 us (0.963)
  the two profiles are of different devices: /device:TPU:4 before, /device:TPU:15 now
where the time goes in v3:
time: 46.9 us; the launch traced here: 46.8 us
  Pallas kernels  35.7 us (76%)
  starting transfers between devices  4.77 us (10%)
  other arithmetic  3.09 us (7%)
  waiting for transfers between devices  2.91 us (6%)
    pallas_call x1, Pallas kernels, body(): pl.pallas_call(functools.partial(late_kernel, slots=slots, heads=heads, c...  23.2 us
    pallas_call x1, Pallas kernels, body(): pl.pallas_call(functools.partial(early_kernel, slots=slots, heads=heads,...  6.5 us
    pallas_call x1, Pallas kernels, body(): pl.pallas_call(functools.partial(join_kernel, slots=slots, step_rows=step...  5.95 us
    ppermute x2, starting transfers between devices, body(): lax.ppermute((far_out, far_stat), 'group', swap_pairs(groups))  2.41 us
    reduce_sum x1, other arithmetic, body(): jnp.sum(wide_q * wide_q, axis=1)  2.41 us
    ppermute x1, waiting for transfers between devices, body(): squares = squares + lax.ppermute(squares, 'tensor', swap_pairs(tensors))  2.2 us
    ppermute x1, starting transfers between devices, body(): far_squares = [lax.ppermute(squares, 'group', swap_pairs(groups))]  1.29 us
  transfers between devices with their start and end apart: 5, of which 2 were waited for; matrix products, arithmetic and copies ran while one was open for 7% of the time, Pallas kernels for 50%

profile of v3, /device:TPU:15, one launch (start us, length us, event | category | flops | bytes accessed | tf_op | source)
XLA Modules:
  0.0 46.8 jit_solution(17042212546121223431)
XLA Ops:
  0.0 0.0 copy-start
  0.0 0.0 copy-start.3
  0.0 0.0 copy-start.4
  0.0 0.0 copy-start.1
  0.0 0.0 copy-start.2
  0.0 0.7 %collective-permute-start.2 = (bf16[512,2560]{1,0:T(8,128)(2,1)}, bf16[512,2560]{1,0:T(8,128)(2,1)}, u32[]{:S(2)}, u32[]{:S(2)}) collective-permute-start(bf16[512,2560]{1,0:T(8,128)(2,1)} %refs_1_.1), channel_id=1, source_target_pairs={{0,2},{2,0},{4,6},{6,4},{8,10},{10,8},{12,14},{14,12},{16,18},{18,... | collective-permute-start | bytes 7864328 | tf_op jit(solution)/shard_map/ppermute | solution.py:359
  0.8 2.4 %multiply_reduce_fusion.1 = f32[512]{0:T(512)S(1)} fusion(bf16[512,2560]{1,0:T(8,128)(2,1)} %refs_1_.1), kind=kLoop, calls=%fused_computation.1 | loop fusion | flops 3931648 | bytes 2623488 | tf_op jit(solution)/shard_map/reduce_sum | solution.py:362
  3.2 0.0 copy-done
  3.2 0.6 %multiply_reduce_fusion = f32[512]{0:T(512)S(1)} fusion(bf16[512,2560]{1,0:T(8,128)(2,1)S(1)} %copy-done), kind=kLoop, calls=%fused_computation | loop fusion | flops 3931648 | bytes 2623488 | tf_op jit(solution)/shard_map/reduce_sum | solution.py:362
  3.8 0.3 collective-permute-start
  4.1 2.2 %collective-permute-done = f32[2,512]{1,0:T(2,128)S(1)} collective-permute-done((f32[2,512]{1,0:T(2,128)S(1)}, f32[2,512]{1,0:T(2,128)S(1)}, u32[]{:S(2)}, u32[]{:S(2)}) %collective-permute-start) | collective-permute-done | bytes 4128 | tf_op jit(solution)/shard_map/ppermute | solution.py:364
  6.3 1.3 %collective-permute-start.1 = (f32[2,512]{1,0:T(2,128)S(1)}, f32[2,512]{1,0:T(2,128)S(1)}, u32[]{:S(2)}, u32[]{:S(2)}) collective-permute-start(f32[2,512]{1,0:T(2,128)S(1)} %fusion.refs_0_), channel_id=1, source_target_pairs={{0,2},{2,0},{4,6},{6,4},{8,10},{10,8},{12,14},{14,12},{16,18},{18,... | collective-permute-start | bytes 12296 | tf_op jit(solution)/shard_map/ppermute | solution.py:368
  7.6 0.0 copy-done.3
  7.6 0.0 copy-done.4
  7.6 0.1 pad_add_fusion.facts_ref
  7.7 0.0 copy-done.1
  7.7 0.0 copy-done.2
  7.7 0.7 %collective-permute-done.1.refs_1_ = f32[2,512]{1,0:T(2,128)S(1)} collective-permute-done((f32[2,512]{1,0:T(2,128)S(1)}, f32[2,512]{1,0:T(2,128)S(1)}, u32[]{:S(2)}, u32[]{:S(2)}) %collective-permute-start.1) | collective-permute-done | bytes 4128 | tf_op jit(solution)/shard_map/ppermute | solution.py:368
  8.4 0.0 collective-permute-done.2.refs_3_
  8.4 6.5 %early_attention.1 = (bf16[512,2560]{1,0:T(8,128)(2,1)}, f32[512,128]{1,0:T(8,128)S(1)}, bf16[512,2560]{1,0:T(8,128)(2,1)}, f32[512,128]{1,0:T(8,128)S(1)}) custom-call(s32[33]{0:T(128)S(1)} %pad_add_fusion.facts_ref, f32[2,512]{1,0:T(2,128)S(1)} %fusion.refs_0_, f32[2,512]{1,0:T(2,128)S(1)} %collective-permute-done.1.refs_1_, bf16[512,2560]{1,0:T(8,128)(2,1)} %refs_1_.1, ...), custom_call_target="tpu_custom_call" | custom-call | flops 4026531840 | bytes 7864320 | tf_op jit(solution)/shard_map/early_attention/pallas_call | solution.py:403
  15.0 2.3 %collective-permute-start.3 = (bf16[512,2560]{1,0:T(8,128)(2,1)}, bf16[512,2560]{1,0:T(8,128)(2,1)S(1)}, u32[]{:S(2)}, u32[]{:S(2)}) collective-permute-start(bf16[512,2560]{1,0:T(8,128)(2,1)} %get-tuple-element.15), channel_id=1, source_target_pairs={{0,2},{2,0},{4,6},{6,4},{8,10},{10,8},{12,14},{14,12},{16,18},{18,... | collective-permute-start | bytes 7864328 | tf_op jit(solution)/shard_map/ppermute | solution.py:413
  17.3 0.1 collective-permute-start.4
  17.4 23.2 %late_attention.1 = (bf16[512,2560]{1,0:T(8,128)(2,1)}, f32[512,128]{1,0:T(8,128)S(1)}) custom-call(s32[33]{0:T(128)S(1)} %pad_add_fusion.facts_ref, f32[2,512]{1,0:T(2,128)S(1)} %fusion.refs_0_, bf16[512,2560]{1,0:T(8,128)(2,1)} %refs_1_.1, bf16[896,2560]{1,0:T(8,128)(2,1)} %refs_2_.3, ...), custom_call_target="tpu_custom_call", output_to_operand_aliasing={{0}: (9, {}), {1}: (10, {})} | custom-call | flops 4026531840 | bytes 7864320 | tf_op jit(solution)/shard_map/late_attention/pallas_call | solution.py:415
  40.6 0.0 collective-permute-done.4.far_stat_any
  40.6 0.0 collective-permute-done.3.far_any
  40.6 5.9 %join_parts.1 = bf16[512,2560]{1,0:T(8,128)(2,1)} custom-call(s32[33]{0:T(128)S(1)} %pad_add_fusion.facts_ref, bf16[512,2560]{1,0:T(8,128)(2,1)} %get-tuple-element.13.own_any, f32[512,128]{1,0:T(8,128)S(1)} %get-tuple-element.14.stat_any, bf16[512,2560]{1,0:T(8,128)(2,1)S(1)} %collective-permute-done.3.far_any, ...), custom_call_target="tpu_custom_call", output_to_operand_aliasing={{}: (1, {})} | custom-call | tf_op jit(solution)/shard_map/join_parts/pallas_call | solution.py:429
  (4 shorter events, 0.0 us)
Async XLA Ops:
  0.0 3.2 %copy-start = (bf16[512,2560]{1,0:T(8,128)(2,1)S(1)}, bf16[512,2560]{1,0:T(8,128)(2,1)}, u32[]{:S(2)}) copy-start(bf16[512,2560]{1,0:T(8,128)(2,1)} %refs_4_.3) | copy-start | bytes 7864324
  0.0 7.6 %copy-start.3 = (s32[16]{0:T(128)S(1)}, s32[16]{0:T(128)}, u32[]{:S(2)}) copy-start(s32[16]{0:T(128)} %param.17) | copy-start | bytes 196
  0.0 7.6 %copy-start.4 = (s32[16]{0:T(128)S(1)}, s32[16]{0:T(128)}, u32[]{:S(2)}) copy-start(s32[16]{0:T(128)} %param.16) | copy-start | bytes 196
  0.0 7.7 %copy-start.1 = (f32[2560]{0:T(1024)S(1)}, f32[2560]{0:T(1024)}, u32[]{:S(2)}) copy-start(f32[2560]{0:T(1024)} %param.14) | copy-start | bytes 30724
  0.0 7.7 %copy-start.2 = (f32[2560]{0:T(1024)S(1)}, f32[2560]{0:T(1024)}, u32[]{:S(2)}) copy-start(f32[2560]{0:T(1024)} %param.15) | copy-start | bytes 30724
  0.0 8.4 %collective-permute-start.2 = (bf16[512,2560]{1,0:T(8,128)(2,1)}, bf16[512,2560]{1,0:T(8,128)(2,1)}, u32[]{:S(2)}, u32[]{:S(2)}) collective-permute-start(bf16[512,2560]{1,0:T(8,128)(2,1)} %refs_1_.1), channel_id=1, source_target_pairs={{0,2},{2,0},{4,6},{6,4},{8,10},{10,8},{12,14},{14,12},{16,18},{18,... | collective-permute-start | bytes 7864328 | tf_op jit(solution)/shard_map/ppermute | solution.py:359
  3.8 2.5 %collective-permute-start = (f32[2,512]{1,0:T(2,128)S(1)}, f32[2,512]{1,0:T(2,128)S(1)}, u32[]{:S(2)}, u32[]{:S(2)}) collective-permute-start(f32[2,512]{1,0:T(2,128)S(1)} %pad_maximum_fusion), channel_id=1, source_target_pairs={{0,1},{1,0},{2,3},{3,2},{4,5},{5,4},{6,7},{7,6},{8,9},{9,8},{10,11... | collective-permute-start | bytes 12296 | tf_op jit(solution)/shard_map/ppermute | solution.py:364
  6.3 2.1 %collective-permute-start.1 = (f32[2,512]{1,0:T(2,128)S(1)}, f32[2,512]{1,0:T(2,128)S(1)}, u32[]{:S(2)}, u32[]{:S(2)}) collective-permute-start(f32[2,512]{1,0:T(2,128)S(1)} %fusion.refs_0_), channel_id=1, source_target_pairs={{0,2},{2,0},{4,6},{6,4},{8,10},{10,8},{12,14},{14,12},{16,18},{18,... | collective-permute-start | bytes 12296 | tf_op jit(solution)/shard_map/ppermute | solution.py:368
  15.0 25.7 %collective-permute-start.3 = (bf16[512,2560]{1,0:T(8,128)(2,1)}, bf16[512,2560]{1,0:T(8,128)(2,1)S(1)}, u32[]{:S(2)}, u32[]{:S(2)}) collective-permute-start(bf16[512,2560]{1,0:T(8,128)(2,1)} %get-tuple-element.15), channel_id=1, source_target_pairs={{0,2},{2,0},{4,6},{6,4},{8,10},{10,8},{12,14},{14,12},{16,18},{18,... | collective-permute-start | bytes 7864328 | tf_op jit(solution)/shard_map/ppermute | solution.py:413
  17.3 23.3 %collective-permute-start.4 = (f32[512,128]{1,0:T(8,128)S(1)}, f32[512,128]{1,0:T(8,128)S(1)}, u32[]{:S(2)}, u32[]{:S(2)}) collective-permute-start(f32[512,128]{1,0:T(8,128)S(1)} %get-tuple-element.16), channel_id=1, source_target_pairs={{0,2},{2,0},{4,6},{6,4},{8,10},{10,8},{12,14},{14,12},{16,18},{18,... | collective-permute-start | bytes 786440 | tf_op jit(solution)/shard_map/ppermute | solution.py:413

commit v4 on v3

--- a/solution.py
+++ b/solution.py
@@ -51,7 +51,7 @@
 def early_heads(away, heads, slots, fresh):
     result = jnp.int32(0)
     for count in range(1, slots):
-        share = min(heads, 2 * int(round(count * heads / (slots + fresh) / 2)))
+        share = min(heads, 2 * math.ceil((2.25 + count) * heads / (slots + fresh + 2.25) / 2 - 0.05))
         result = jnp.where(away == count, share, result)
     return result
 
@@ -295,51 +295,37 @@
                 copy.wait()
 
 
-def join_kernel(
-    facts_ref, own_any, stat_any, far_any, far_stat_any, out_any,
-    own, far, stat, far_stat, spread, out, in_sems, out_sems, *, slots, step_rows
-):
+def join_kernel(facts_ref, own_any, stat, far, far_stat, out_any, own, out, in_sems, out_sems, *, slots, step_rows):
     away = counts(facts_ref, slots)[4]
-    row_count = own.shape[0]
-    steps = row_count // step_rows
+    steps = own.shape[0] // step_rows
 
     @pl.when(away > 0)
     def _():
         def piece(step):
             return pl.ds(pl.multiple_of(step * step_rows, step_rows), step_rows)
 
-        def copies(step):
-            rows = piece(step)
-            pairs = ((own_any, own), (far_any, far), (stat_any, stat), (far_stat_any, far_stat))
-            return [
-                pltpu.make_async_copy(a.at[rows, :], b.at[rows, :], in_sems.at[i, step]) for i, (a, b) in enumerate(pairs)
-            ]
+        def read(step):
+            return pltpu.make_async_copy(own_any.at[piece(step), :], own.at[piece(step), :], in_sems.at[step])
 
         def write(step):
             return pltpu.make_async_copy(out.at[piece(step), :], out_any.at[piece(step), :], out_sems.at[step])
 
         for step in range(steps):
-            for copy in copies(step):
-                copy.start()
-
-        lane = lax.broadcasted_iota(jnp.int32, spread.shape, 0) * HD
-        column = lax.broadcasted_iota(jnp.int32, spread.shape, 1)
-        spread[...] = ((column >= lane) & (column < lane + HD)).astype(jnp.bfloat16)
+            read(step).start()
 
         def one(step, carry):
-            for copy in copies(step):
-                copy.wait()
             rows = piece(step)
             near, away_stat = stat[rows, :], far_stat[rows, :]
             top = jnp.maximum(near, away_stat)
             own_part = pltpu.roll(near, HD - SUM_LANE, 1) * jnp.exp2(near - top)
             far_part = pltpu.roll(away_stat, HD - SUM_LANE, 1) * jnp.exp2(away_stat - top)
-            known = lax.broadcasted_iota(jnp.int32, near.shape, 1) < own.shape[1] // HD
-            share = jnp.where(known, far_part / (own_part + far_part), 0.0)
-            wide = jnp.dot(share.astype(jnp.bfloat16), spread[...], preferred_element_type=jnp.float32)
-            here = own[rows, :].astype(jnp.float32)
-            there = far[rows, :].astype(jnp.float32)
-            out[rows, :] = (here + wide * (there - here)).astype(jnp.bfloat16)
+            share = far_part / (own_part + far_part)
+            read(step).wait()
+            for head in range(own.shape[1] // HD):
+                cut = slice(head * HD, (head + 1) * HD)
+                here = own[rows, cut].astype(jnp.float32)
+                there = far[rows, cut].astype(jnp.float32)
+                out[rows, cut] = (here + share[:, head : head + 1] * (there - here)).astype(jnp.bfloat16)
             write(step).start()
             return carry
 
@@ -429,12 +415,10 @@
     return pl.pallas_call(
         functools.partial(join_kernel, slots=slots, step_rows=step_rows),
         out_shape=result,
-        in_specs=smem + [anywhere] * 4,
+        in_specs=smem + [anywhere] + [vmem] * 3,
         out_specs=anywhere,
         scratch_shapes=[
-            new_rows, new_rows, stat_space, stat_space,
-            pltpu.VMEM((HD, feature_count), jnp.bfloat16), new_rows,
-            pltpu.SemaphoreType.DMA((4, steps)), pltpu.SemaphoreType.DMA((steps,)),
+            new_rows, new_rows, pltpu.SemaphoreType.DMA((steps,)), pltpu.SemaphoreType.DMA((steps,)),
         ],
         input_output_aliases={1: 0},
         compiler_params=params(24 * 1024 * 1024),

time: 46.9 us -> 44.8 us (0.955)
  the two profiles are of different devices: /device:TPU:15 before, /device:TPU:0 now
where the time goes in v4:
time: 44.8 us
  Pallas kernels  34.9 us (78%)
  starting transfers between devices  3.59 us (8%)
  other arithmetic  3.31 us (7%)
  waiting for transfers between devices  2.6 us (6%)
    pallas_call x1, Pallas kernels, body(): pl.pallas_call(functools.partial(late_kernel, slots=slots, heads=heads, c...  17 us
    pallas_call x1, Pallas kernels, body(): pl.pallas_call(functools.partial(early_kernel, slots=slots, heads=heads,...  12.7 us
    pallas_call x1, Pallas kernels, body(): pl.pallas_call(functools.partial(join_kernel, slots=slots, step_rows=step...  5.19 us
    reduce_sum x1, other arithmetic, body(): jnp.sum(wide_q * wide_q, axis=1)  2.63 us
    ppermute x1, starting transfers between devices, body(): squares = squares + lax.ppermute(squares, 'tensor', swap_pairs(tensors))  2.42 us
    ppermute x1, waiting for transfers between devices, body(): squares = squares + lax.ppermute(squares, 'tensor', swap_pairs(tensors))  1.59 us
    ppermute x1, waiting for transfers between devices, body(): far_squares = [lax.ppermute(squares, 'group', swap_pairs(groups))]  1.01 us
  transfers between devices with their start and end apart: 5, of which 2 were waited for; matrix products, arithmetic and copies ran while one was open for 7% of the time, Pallas kernels for 38%

profile of v4, /device:TPU:0, one launch (start us, length us, event | category | flops | bytes accessed | tf_op | source)
XLA Modules:
  0.0 44.8 jit_solution(10903515310816711379)
XLA Ops:
  0.0 0.0 copy-start
  0.0 0.0 copy-start.3
  0.0 0.0 copy-start.4
  0.0 0.0 copy-start.1
  0.0 0.0 copy-start.2
  0.0 0.5 %collective-permute-start.2 = (bf16[512,2560]{1,0:T(8,128)(2,1)}, bf16[512,2560]{1,0:T(8,128)(2,1)}, u32[]{:S(2)}, u32[]{:S(2)}) collective-permute-start(bf16[512,2560]{1,0:T(8,128)(2,1)} %refs_1_.1), channel_id=1, source_target_pairs={{0,2},{2,0},{4,6},{6,4},{8,10},{10,8},{12,14},{14,12},{16,18},{18,... | collective-permute-start | bytes 7864328 | tf_op jit(solution)/shard_map/ppermute | solution.py:345
  0.5 2.6 %multiply_reduce_fusion.1 = f32[512]{0:T(512)S(1)} fusion(bf16[512,2560]{1,0:T(8,128)(2,1)} %refs_1_.1), kind=kLoop, calls=%fused_computation.1 | loop fusion | flops 3931648 | bytes 2623488 | tf_op jit(solution)/shard_map/reduce_sum | solution.py:348
  3.2 0.0 copy-done
  3.2 0.6 %multiply_reduce_fusion = f32[512]{0:T(512)S(1)} fusion(bf16[512,2560]{1,0:T(8,128)(2,1)S(1)} %copy-done), kind=kLoop, calls=%fused_computation | loop fusion | flops 3931648 | bytes 2623488 | tf_op jit(solution)/shard_map/reduce_sum | solution.py:348
  3.8 2.4 %collective-permute-start = (f32[2,512]{1,0:T(2,128)S(1)}, f32[2,512]{1,0:T(2,128)S(1)}, u32[]{:S(2)}, u32[]{:S(2)}) collective-permute-start(f32[2,512]{1,0:T(2,128)S(1)} %pad_maximum_fusion), channel_id=1, source_target_pairs={{0,1},{1,0},{2,3},{3,2},{4,5},{5,4},{6,7},{7,6},{8,9},{9,8},{10,11... | collective-permute-start | bytes 12296 | tf_op jit(solution)/shard_map/ppermute | solution.py:350
  6.2 1.6 %collective-permute-done = f32[2,512]{1,0:T(2,128)S(1)} collective-permute-done((f32[2,512]{1,0:T(2,128)S(1)}, f32[2,512]{1,0:T(2,128)S(1)}, u32[]{:S(2)}, u32[]{:S(2)}) %collective-permute-start) | collective-permute-done | bytes 4128 | tf_op jit(solution)/shard_map/ppermute | solution.py:350
  7.8 0.1 collective-permute-start.1
  7.9 0.0 copy-done.3
  7.9 0.0 copy-done.4
  7.9 0.1 pad_add_fusion.facts_ref
  8.0 0.0 copy-done.1
  8.0 0.0 copy-done.2
  8.0 1.0 %collective-permute-done.1.refs_1_ = f32[2,512]{1,0:T(2,128)S(1)} collective-permute-done((f32[2,512]{1,0:T(2,128)S(1)}, f32[2,512]{1,0:T(2,128)S(1)}, u32[]{:S(2)}, u32[]{:S(2)}) %collective-permute-start.1) | collective-permute-done | bytes 4128 | tf_op jit(solution)/shard_map/ppermute | solution.py:354
  9.0 0.0 collective-permute-done.2.refs_3_
  9.0 12.7 %early_attention.1 = (bf16[512,2560]{1,0:T(8,128)(2,1)}, f32[512,128]{1,0:T(8,128)S(1)}, bf16[512,2560]{1,0:T(8,128)(2,1)}, f32[512,128]{1,0:T(8,128)S(1)}) custom-call(s32[33]{0:T(128)S(1)} %pad_add_fusion.facts_ref, f32[2,512]{1,0:T(2,128)S(1)} %fusion.refs_0_, f32[2,512]{1,0:T(2,128)S(1)} %collective-permute-done.1.refs_1_, bf16[512,2560]{1,0:T(8,128)(2,1)} %refs_1_.1, ...), custom_call_target="tpu_custom_call" | custom-call | flops 4026531840 | bytes 7864320 | tf_op jit(solution)/shard_map/early_attention/pallas_call | solution.py:389
  21.7 0.1 collective-permute-start.3
  21.8 0.5 %collective-permute-start.4 = (f32[512,128]{1,0:T(8,128)S(1)}, f32[512,128]{1,0:T(8,128)S(1)}, u32[]{:S(2)}, u32[]{:S(2)}) collective-permute-start(f32[512,128]{1,0:T(8,128)S(1)} %get-tuple-element.16), channel_id=1, source_target_pairs={{0,2},{2,0},{4,6},{6,4},{8,10},{10,8},{12,14},{14,12},{16,18},{18,... | collective-permute-start | bytes 786440 | tf_op jit(solution)/shard_map/ppermute | solution.py:399
  22.3 17.0 %late_attention.1 = (bf16[512,2560]{1,0:T(8,128)(2,1)}, f32[512,128]{1,0:T(8,128)S(1)}) custom-call(s32[33]{0:T(128)S(1)} %pad_add_fusion.facts_ref, f32[2,512]{1,0:T(2,128)S(1)} %fusion.refs_0_, bf16[512,2560]{1,0:T(8,128)(2,1)} %refs_1_.1, bf16[896,2560]{1,0:T(8,128)(2,1)} %refs_2_.3, ...), custom_call_target="tpu_custom_call", output_to_operand_aliasing={{0}: (9, {}), {1}: (10, {})} | custom-call | flops 4026531840 | bytes 7864320 | tf_op jit(solution)/shard_map/late_attention/pallas_call | solution.py:401
  39.4 0.0 collective-permute-done.4.far_stat
  39.4 0.0 collective-permute-done.3.far
  39.4 5.2 %join_parts.1 = bf16[512,2560]{1,0:T(8,128)(2,1)} custom-call(s32[33]{0:T(128)S(1)} %pad_add_fusion.facts_ref, bf16[512,2560]{1,0:T(8,128)(2,1)} %get-tuple-element.13.own_any, f32[512,128]{1,0:T(8,128)S(1)} %get-tuple-element.14.stat, bf16[512,2560]{1,0:T(8,128)(2,1)S(1)} %collective-permute-done.3.far, ...), custom_call_target="tpu_custom_call", output_to_operand_aliasing={{}: (1, {})} | custom-call | tf_op jit(solution)/shard_map/join_parts/pallas_call | solution.py:415
  (4 shorter events, 0.0 us)
Async XLA Ops:
  0.0 3.2 %copy-start = (bf16[512,2560]{1,0:T(8,128)(2,1)S(1)}, bf16[512,2560]{1,0:T(8,128)(2,1)}, u32[]{:S(2)}) copy-start(bf16[512,2560]{1,0:T(8,128)(2,1)} %refs_4_.3) | copy-start | bytes 7864324
  0.0 7.9 %copy-start.3 = (s32[16]{0:T(128)S(1)}, s32[16]{0:T(128)}, u32[]{:S(2)}) copy-start(s32[16]{0:T(128)} %param.17) | copy-start | bytes 196
  0.0 7.9 %copy-start.4 = (s32[16]{0:T(128)S(1)}, s32[16]{0:T(128)}, u32[]{:S(2)}) copy-start(s32[16]{0:T(128)} %param.16) | copy-start | bytes 196
  0.0 8.0 %copy-start.1 = (f32[2560]{0:T(1024)S(1)}, f32[2560]{0:T(1024)}, u32[]{:S(2)}) copy-start(f32[2560]{0:T(1024)} %param.14) | copy-start | bytes 30724
  0.0 8.0 %copy-start.2 = (f32[2560]{0:T(1024)S(1)}, f32[2560]{0:T(1024)}, u32[]{:S(2)}) copy-start(f32[2560]{0:T(1024)} %param.15) | copy-start | bytes 30724
  0.0 9.0 %collective-permute-start.2 = (bf16[512,2560]{1,0:T(8,128)(2,1)}, bf16[512,2560]{1,0:T(8,128)(2,1)}, u32[]{:S(2)}, u32[]{:S(2)}) collective-permute-start(bf16[512,2560]{1,0:T(8,128)(2,1)} %refs_1_.1), channel_id=1, source_target_pairs={{0,2},{2,0},{4,6},{6,4},{8,10},{10,8},{12,14},{14,12},{16,18},{18,... | collective-permute-start | bytes 7864328 | tf_op jit(solution)/shard_map/ppermute | solution.py:345
  3.8 4.0 %collective-permute-start = (f32[2,512]{1,0:T(2,128)S(1)}, f32[2,512]{1,0:T(2,128)S(1)}, u32[]{:S(2)}, u32[]{:S(2)}) collective-permute-start(f32[2,512]{1,0:T(2,128)S(1)} %pad_maximum_fusion), channel_id=1, source_target_pairs={{0,1},{1,0},{2,3},{3,2},{4,5},{5,4},{6,7},{7,6},{8,9},{9,8},{10,11... | collective-permute-start | bytes 12296 | tf_op jit(solution)/shard_map/ppermute | solution.py:350
  7.8 1.2 %collective-permute-start.1 = (f32[2,512]{1,0:T(2,128)S(1)}, f32[2,512]{1,0:T(2,128)S(1)}, u32[]{:S(2)}, u32[]{:S(2)}) collective-permute-start(f32[2,512]{1,0:T(2,128)S(1)} %fusion.refs_0_), channel_id=1, source_target_pairs={{0,2},{2,0},{4,6},{6,4},{8,10},{10,8},{12,14},{14,12},{16,18},{18,... | collective-permute-start | bytes 12296 | tf_op jit(solution)/shard_map/ppermute | solution.py:354
  21.7 17.6 %collective-permute-start.3 = (bf16[512,2560]{1,0:T(8,128)(2,1)}, bf16[512,2560]{1,0:T(8,128)(2,1)S(1)}, u32[]{:S(2)}, u32[]{:S(2)}) collective-permute-start(bf16[512,2560]{1,0:T(8,128)(2,1)} %get-tuple-element.15), channel_id=1, source_target_pairs={{0,2},{2,0},{4,6},{6,4},{8,10},{10,8},{12,14},{14,12},{16,18},{18,... | collective-permute-start | bytes 7864328 | tf_op jit(solution)/shard_map/ppermute | solution.py:399
  21.8 17.5 %collective-permute-start.4 = (f32[512,128]{1,0:T(8,128)S(1)}, f32[512,128]{1,0:T(8,128)S(1)}, u32[]{:S(2)}, u32[]{:S(2)}) collective-permute-start(f32[512,128]{1,0:T(8,128)S(1)} %get-tuple-element.16), channel_id=1, source_target_pairs={{0,2},{2,0},{4,6},{6,4},{8,10},{10,8},{12,14},{14,12},{16,18},{18,... | collective-permute-start | bytes 786440 | tf_op jit(solution)/shard_map/ppermute | solution.py:399

commit v5 on v4

--- a/solution.py
+++ b/solution.py
@@ -98,14 +98,24 @@
                     column = jnp.where(self.lane < self.tail, column, NEGATIVE)
                 self.scores[slot][:, start : start + CB] = column
                 top = column if top is None else jnp.maximum(top, column)
+            yield
         self.tops[slot][...] = jnp.broadcast_to(jnp.max(top, axis=1, keepdims=True), (self.rows, HD))
 
     def soften(self, head, slot):
         top = self.tops[slot][...]
-        for start in range(0, self.total, CB):
-            column = self.scores[slot][:, start : start + CB]
-            self.weights[slot][:, start : start + CB] = jnp.exp2(column - top).astype(jnp.bfloat16)
+        for begin in range(0, self.total, KEYS):
+            for start in range(begin, min(begin + KEYS, self.total), CB):
+                column = self.scores[slot][:, start : start + CB]
+                self.weights[slot][:, start : start + CB] = jnp.exp2(column - top).astype(jnp.bfloat16)
+            yield
         pltpu.store(self.stat, top, mask=self.lane == head)
+
+    def alternate(self, *works):
+        works = list(works)
+        while works:
+            for work in list(works):
+                if next(work, self) is self:
+                    works.remove(work)
 
     def mix(self, head, target, lane, slot):
         cut = lanes(head)
@@ -122,39 +132,28 @@
 
     def run(self, first, last, spare, ready, done, finish=None):
         ready(first, True)
-        self.score(first, 0)
-        count = last - first
-        paired = lax.rem(count, 2) == 0
+        self.alternate(self.score(first, 0))
 
         def step(index, carry):
             head = first + 2 * index
             second = jnp.minimum(head + 1, last - 1)
             later = jnp.minimum(head + 2, last - 1)
-            begun = index > 0
-            before = jnp.maximum(head - 1, first)
+            paired = head + 1 < last
             ready(head + 1, False)
             ready(head + 2, False)
-            self.score(second, 1)
-            self.soften(head, 0)
-            self.mix(before, jnp.where(begun, before, spare), jnp.where(begun, before, SUM_LANE - 1), 1)
-            self.score(later, 0)
-            self.soften(second, 1)
+            self.alternate(self.score(second, 1), self.soften(head, 0))
             self.mix(head, head, head, 0)
+            self.alternate(self.score(later, 0), self.soften(second, 1))
+            self.mix(second, jnp.where(paired, second, spare), second, 1)
             done(head).start()
 
-            @pl.when(begun)
+            @pl.when(paired)
             def _():
-                done(before).start()
+                done(second).start()
 
             return carry
 
-        lax.fori_loop(0, lax.shift_right_logical(count + 1, 1), step, 0)
-        self.mix(last - 1, jnp.where(paired, last - 1, spare), last - 1, 1)
-
-        @pl.when(paired)
-        def _():
-            done(last - 1).start()
-
+        lax.fori_loop(0, lax.shift_right_logical(last - first + 1, 1), step, 0)
         if finish is not None:
             finish()
         lax.fori_loop(first, last, lambda head, carry: (done(head).wait(), carry)[1], 0)

time: 44.8 us -> 45.2 us (level)
  starting transfers between devices: 3.59 us -> 6.42 us
  Pallas kernels: 34.9 us -> 32.4 us
    pallas_call x1, Pallas kernels: 5.19 us -> 0.71 us  [body(): pl.pallas_call(functools.partial(join_kernel, slots=slots, step_rows=step...]
    pallas_call x1, Pallas kernels: 12.7 us -> 16 us  [body(): pl.pallas_call(functools.partial(early_kernel, slots=slots, heads=heads,...]
    ppermute x2, starting transfers between devices: 0.57 us -> 3.4 us  [body(): lax.ppermute((far_out, far_stat), 'group', swap_pairs(groups))]
    pallas_call x1, Pallas kernels: 17 us -> 15.7 us  [body(): pl.pallas_call(functools.partial(late_kernel, slots=slots, heads=heads, c...]
  transfers between devices with their start and end apart: 5 -> 5, of which waited for: 2 -> 2; matrix products, arithmetic and copies ran while one was open for 7% -> 7% of each run, Pallas kernels for 38% -> 35%
where the time goes in v5:
time: 45.2 us; the launch traced here: 45.1 us
  Pallas kernels  32.4 us (72%)
  starting transfers between devices  6.42 us (14%)
  other arithmetic  3.31 us (7%)
  waiting for transfers between devices  2.6 us (6%)
    pallas_call x1, Pallas kernels, body(): pl.pallas_call(functools.partial(early_kernel, slots=slots, heads=heads,...  16 us
    pallas_call x1, Pallas kernels, body(): pl.pallas_call(functools.partial(late_kernel, slots=slots, heads=heads, c...  15.7 us
    ppermute x2, starting transfers between devices, body(): lax.ppermute((far_out, far_stat), 'group', swap_pairs(groups))  3.4 us
    reduce_sum x1, other arithmetic, body(): jnp.sum(wide_q * wide_q, axis=1)  2.63 us
    ppermute x1, starting transfers between devices, body(): squares = squares + lax.ppermute(squares, 'tensor', swap_pairs(tensors))  2.42 us
    ppermute x1, waiting for transfers between devices, body(): squares = squares + lax.ppermute(squares, 'tensor', swap_pairs(tensors))  1.59 us
    ppermute x1, waiting for transfers between devices, body(): far_squares = [lax.ppermute(squares, 'group', swap_pairs(groups))]  1.01 us
  transfers between devices with their start and end apart: 5, of which 2 were waited for; matrix products, arithmetic and copies ran while one was open for 7% of the time, Pallas kernels for 35%

profile of v5, /device:TPU:0, one launch (start us, length us, event | category | flops | bytes accessed | tf_op | source)
XLA Modules:
  0.0 45.1 jit_solution(8171200709432360355)
XLA Ops:
  0.0 0.0 copy-start
  0.0 0.0 copy-start.3
  0.0 0.0 copy-start.4
  0.0 0.0 copy-start.1
  0.0 0.0 copy-start.2
  0.0 0.5 %collective-permute-start.2 = (bf16[512,2560]{1,0:T(8,128)(2,1)}, bf16[512,2560]{1,0:T(8,128)(2,1)}, u32[]{:S(2)}, u32[]{:S(2)}) collective-permute-start(bf16[512,2560]{1,0:T(8,128)(2,1)} %refs_1_.1), channel_id=1, source_target_pairs={{0,2},{2,0},{4,6},{6,4},{8,10},{10,8},{12,14},{14,12},{16,18},{18,... | collective-permute-start | bytes 7864328 | tf_op jit(solution)/shard_map/ppermute | solution.py:344
  0.5 2.6 %multiply_reduce_fusion.1 = f32[512]{0:T(512)S(1)} fusion(bf16[512,2560]{1,0:T(8,128)(2,1)} %refs_1_.1), kind=kLoop, calls=%fused_computation.1 | loop fusion | flops 3931648 | bytes 2623488 | tf_op jit(solution)/shard_map/reduce_sum | solution.py:347
  3.2 0.0 copy-done
  3.2 0.6 %multiply_reduce_fusion = f32[512]{0:T(512)S(1)} fusion(bf16[512,2560]{1,0:T(8,128)(2,1)S(1)} %copy-done), kind=kLoop, calls=%fused_computation | loop fusion | flops 3931648 | bytes 2623488 | tf_op jit(solution)/shard_map/reduce_sum | solution.py:347
  3.8 2.4 %collective-permute-start = (f32[2,512]{1,0:T(2,128)S(1)}, f32[2,512]{1,0:T(2,128)S(1)}, u32[]{:S(2)}, u32[]{:S(2)}) collective-permute-start(f32[2,512]{1,0:T(2,128)S(1)} %pad_maximum_fusion), channel_id=1, source_target_pairs={{0,1},{1,0},{2,3},{3,2},{4,5},{5,4},{6,7},{7,6},{8,9},{9,8},{10,11... | collective-permute-start | bytes 12296 | tf_op jit(solution)/shard_map/ppermute | solution.py:349
  6.2 1.6 %collective-permute-done = f32[2,512]{1,0:T(2,128)S(1)} collective-permute-done((f32[2,512]{1,0:T(2,128)S(1)}, f32[2,512]{1,0:T(2,128)S(1)}, u32[]{:S(2)}, u32[]{:S(2)}) %collective-permute-start) | collective-permute-done | bytes 4128 | tf_op jit(solution)/shard_map/ppermute | solution.py:349
  7.8 0.1 collective-permute-start.1
  7.9 0.0 copy-done.3
  7.9 0.0 copy-done.4
  7.9 0.1 pad_add_fusion.facts_ref
  8.0 0.0 copy-done.1
  8.0 0.0 copy-done.2
  8.0 1.0 %collective-permute-done.1.refs_1_ = f32[2,512]{1,0:T(2,128)S(1)} collective-permute-done((f32[2,512]{1,0:T(2,128)S(1)}, f32[2,512]{1,0:T(2,128)S(1)}, u32[]{:S(2)}, u32[]{:S(2)}) %collective-permute-start.1) | collective-permute-done | bytes 4128 | tf_op jit(solution)/shard_map/ppermute | solution.py:353
  9.0 0.0 collective-permute-done.2.refs_3_
  9.0 16.0 %early_attention.1 = (bf16[512,2560]{1,0:T(8,128)(2,1)}, f32[512,128]{1,0:T(8,128)S(1)}, bf16[512,2560]{1,0:T(8,128)(2,1)}, f32[512,128]{1,0:T(8,128)S(1)}) custom-call(s32[33]{0:T(128)S(1)} %pad_add_fusion.facts_ref, f32[2,512]{1,0:T(2,128)S(1)} %fusion.refs_0_, f32[2,512]{1,0:T(2,128)S(1)} %collective-permute-done.1.refs_1_, bf16[512,2560]{1,0:T(8,128)(2,1)} %refs_1_.1, ...), custom_call_target="tpu_custom_call" | custom-call | flops 4026531840 | bytes 7864320 | tf_op jit(solution)/shard_map/early_attention/pallas_call | solution.py:388
  25.0 3.3 %collective-permute-start.3 = (bf16[512,2560]{1,0:T(8,128)(2,1)}, bf16[512,2560]{1,0:T(8,128)(2,1)S(1)}, u32[]{:S(2)}, u32[]{:S(2)}) collective-permute-start(bf16[512,2560]{1,0:T(8,128)(2,1)} %get-tuple-element.15), channel_id=1, source_target_pairs={{0,2},{2,0},{4,6},{6,4},{8,10},{10,8},{12,14},{14,12},{16,18},{18,... | collective-permute-start | bytes 7864328 | tf_op jit(solution)/shard_map/ppermute | solution.py:398
  28.4 0.1 collective-permute-start.4
  28.4 15.7 %late_attention.1 = (bf16[512,2560]{1,0:T(8,128)(2,1)}, f32[512,128]{1,0:T(8,128)S(1)}) custom-call(s32[33]{0:T(128)S(1)} %pad_add_fusion.facts_ref, f32[2,512]{1,0:T(2,128)S(1)} %fusion.refs_0_, bf16[512,2560]{1,0:T(8,128)(2,1)} %refs_1_.1, bf16[896,2560]{1,0:T(8,128)(2,1)} %refs_2_.3, ...), custom_call_target="tpu_custom_call", output_to_operand_aliasing={{0}: (9, {}), {1}: (10, {})} | custom-call | flops 4026531840 | bytes 7864320 | tf_op jit(solution)/shard_map/late_attention/pallas_call | solution.py:400
  44.2 0.0 collective-permute-done.4.far_stat
  44.2 0.0 collective-permute-done.3.far
  44.2 0.7 %join_parts.1 = bf16[512,2560]{1,0:T(8,128)(2,1)} custom-call(s32[33]{0:T(128)S(1)} %pad_add_fusion.facts_ref, bf16[512,2560]{1,0:T(8,128)(2,1)} %get-tuple-element.13.own_any, f32[512,128]{1,0:T(8,128)S(1)} %get-tuple-element.14.stat, bf16[512,2560]{1,0:T(8,128)(2,1)S(1)} %collective-permute-done.3.far, ...), custom_call_target="tpu_custom_call", output_to_operand_aliasing={{}: (1, {})} | custom-call | tf_op jit(solution)/shard_map/join_parts/pallas_call | solution.py:414
  (4 shorter events, 0.0 us)
Async XLA Ops:
  0.0 3.2 %copy-start = (bf16[512,2560]{1,0:T(8,128)(2,1)S(1)}, bf16[512,2560]{1,0:T(8,128)(2,1)}, u32[]{:S(2)}) copy-start(bf16[512,2560]{1,0:T(8,128)(2,1)} %refs_4_.3) | copy-start | bytes 7864324
  0.0 7.9 %copy-start.3 = (s32[16]{0:T(128)S(1)}, s32[16]{0:T(128)}, u32[]{:S(2)}) copy-start(s32[16]{0:T(128)} %param.17) | copy-start | bytes 196
  0.0 7.9 %copy-start.4 = (s32[16]{0:T(128)S(1)}, s32[16]{0:T(128)}, u32[]{:S(2)}) copy-start(s32[16]{0:T(128)} %param.16) | copy-start | bytes 196
  0.0 8.0 %copy-start.1 = (f32[2560]{0:T(1024)S(1)}, f32[2560]{0:T(1024)}, u32[]{:S(2)}) copy-start(f32[2560]{0:T(1024)} %param.14) | copy-start | bytes 30724
  0.0 8.0 %copy-start.2 = (f32[2560]{0:T(1024)S(1)}, f32[2560]{0:T(1024)}, u32[]{:S(2)}) copy-start(f32[2560]{0:T(1024)} %param.15) | copy-start | bytes 30724
  0.0 9.0 %collective-permute-start.2 = (bf16[512,2560]{1,0:T(8,128)(2,1)}, bf16[512,2560]{1,0:T(8,128)(2,1)}, u32[]{:S(2)}, u32[]{:S(2)}) collective-permute-start(bf16[512,2560]{1,0:T(8,128)(2,1)} %refs_1_.1), channel_id=1, source_target_pairs={{0,2},{2,0},{4,6},{6,4},{8,10},{10,8},{12,14},{14,12},{16,18},{18,... | collective-permute-start | bytes 7864328 | tf_op jit(solution)/shard_map/ppermute | solution.py:344
  3.8 4.0 %collective-permute-start = (f32[2,512]{1,0:T(2,128)S(1)}, f32[2,512]{1,0:T(2,128)S(1)}, u32[]{:S(2)}, u32[]{:S(2)}) collective-permute-start(f32[2,512]{1,0:T(2,128)S(1)} %pad_maximum_fusion), channel_id=1, source_target_pairs={{0,1},{1,0},{2,3},{3,2},{4,5},{5,4},{6,7},{7,6},{8,9},{9,8},{10,11... | collective-permute-start | bytes 12296 | tf_op jit(solution)/shard_map/ppermute | solution.py:349
  7.8 1.2 %collective-permute-start.1 = (f32[2,512]{1,0:T(2,128)S(1)}, f32[2,512]{1,0:T(2,128)S(1)}, u32[]{:S(2)}, u32[]{:S(2)}) collective-permute-start(f32[2,512]{1,0:T(2,128)S(1)} %fusion.refs_0_), channel_id=1, source_target_pairs={{0,2},{2,0},{4,6},{6,4},{8,10},{10,8},{12,14},{14,12},{16,18},{18,... | collective-permute-start | bytes 12296 | tf_op jit(solution)/shard_map/ppermute | solution.py:353
  25.0 19.2 %collective-permute-start.3 = (bf16[512,2560]{1,0:T(8,128)(2,1)}, bf16[512,2560]{1,0:T(8,128)(2,1)S(1)}, u32[]{:S(2)}, u32[]{:S(2)}) collective-permute-start(bf16[512,2560]{1,0:T(8,128)(2,1)} %get-tuple-element.15), channel_id=1, source_target_pairs={{0,2},{2,0},{4,6},{6,4},{8,10},{10,8},{12,14},{14,12},{16,18},{18,... | collective-permute-start | bytes 7864328 | tf_op jit(solution)/shard_map/ppermute | solution.py:398
  28.4 15.8 %collective-permute-start.4 = (f32[512,128]{1,0:T(8,128)S(1)}, f32[512,128]{1,0:T(8,128)S(1)}, u32[]{:S(2)}, u32[]{:S(2)}) collective-permute-start(f32[512,128]{1,0:T(8,128)S(1)} %get-tuple-element.16), channel_id=1, source_target_pairs={{0,2},{2,0},{4,6},{6,4},{8,10},{10,8},{12,14},{14,12},{16,18},{18,... | collective-permute-start | bytes 786440 | tf_op jit(solution)/shard_map/ppermute | solution.py:398

commit v6 on v4

--- a/solution.py
+++ b/solution.py
@@ -104,7 +104,7 @@
         top = self.tops[slot][...]
         for start in range(0, self.total, CB):
             column = self.scores[slot][:, start : start + CB]
-            self.weights[slot][:, start : start + CB] = jnp.exp2(column - top).astype(jnp.bfloat16)
+            self.weights[slot][:, start : start + CB] = jnp.exp2((column - top).astype(jnp.bfloat16))
         pltpu.store(self.stat, top, mask=self.lane == head)
 
     def mix(self, head, target, lane, slot):
@@ -121,8 +121,9 @@
         pltpu.store(self.stat, totals, mask=self.lane == lane + SUM_LANE)
 
     def run(self, first, last, spare, ready, done, finish=None):
-        ready(first, True)
+        ready(first, "keys")
         self.score(first, 0)
+        ready(first, "values")
         count = last - first
         paired = lax.rem(count, 2) == 0
 
@@ -132,8 +133,8 @@
             later = jnp.minimum(head + 2, last - 1)
             begun = index > 0
             before = jnp.maximum(head - 1, first)
-            ready(head + 1, False)
-            ready(head + 2, False)
+            ready(head + 1)
+            ready(head + 2)
             self.score(second, 1)
             self.soften(head, 0)
             self.mix(before, jnp.where(begun, before, spare), jnp.where(begun, before, SUM_LANE - 1), 1)
@@ -174,8 +175,9 @@
 
     def start(first, last, between):
         def one(part, carry):
-            for copy in copies(part):
-                copy.start()
+            pieces = copies(part)
+            for index in (0, 1, 3, 2, 4) if len(pieces) > 3 else (0, 1, 2):
+                pieces[index].start()
             return carry
 
         one(first // chunk, 0)
@@ -183,15 +185,20 @@
         lax.fori_loop(first // chunk + 1, (last + chunk - 1) // chunk, one, 0)
 
     def ready(first, last):
-        def wait(head, at_start):
-            if at_start:
-                wanted = True
-            else:
-                wanted = (head < last) & (lax.rem(head, chunk) == 0)
-
-            @pl.when(wanted)
+        def wait(head, kind=None):
+            pieces = copies(head // chunk)
+            if kind == "keys":
+                for index in (0, 1, 3)[: len(pieces) // 2 + 1 if len(pieces) > 3 else 2]:
+                    pieces[index].wait()
+                return
+            if kind == "values":
+                for index in (2, 4)[: 2 if len(pieces) > 3 else 1]:
+                    pieces[index].wait()
+                return
+
+            @pl.when((head < last) & (lax.rem(head, chunk) == 0))
             def _():
-                for copy in copies(head // chunk):
+                for copy in pieces:
                     copy.wait()
 
         return wait

time: 44.8 us -> 45.7 us (1.020)
  Pallas kernels: 34.9 us -> 35.7 us
    pallas_call x1, Pallas kernels: 12.7 us -> 19.4 us  [body(): pl.pallas_call(functools.partial(early_kernel, slots=slots, heads=heads,...]
    pallas_call x1, Pallas kernels: 17 us -> 11.2 us  [body(): pl.pallas_call(functools.partial(late_kernel, slots=slots, heads=heads, c...]
  transfers between devices with their start and end apart: 5 -> 5, of which waited for: 2 -> 2; matrix products, arithmetic and copies ran while one was open for 7% -> 7% of each run, Pallas kernels for 38% -> 25%
where the time goes in v6:
time: 45.7 us; the launch traced here: 45.6 us
  Pallas kernels  35.7 us (78%)
  starting transfers between devices  3.59 us (8%)
  other arithmetic  3.31 us (7%)
  waiting for transfers between devices  2.6 us (6%)
    pallas_call x1, Pallas kernels, body(): pl.pallas_call(functools.partial(early_kernel, slots=slots, heads=heads,...  19.4 us
    pallas_call x1, Pallas kernels, body(): pl.pallas_call(functools.partial(late_kernel, slots=slots, heads=heads, c...  11.2 us
    pallas_call x1, Pallas kernels, body(): pl.pallas_call(functools.partial(join_kernel, slots=slots, step_rows=step...  5.19 us
    reduce_sum x1, other arithmetic, body(): jnp.sum(wide_q * wide_q, axis=1)  2.63 us
    ppermute x1, starting transfers between devices, body(): squares = squares + lax.ppermute(squares, 'tensor', swap_pairs(tensors))  2.42 us
    ppermute x1, waiting for transfers between devices, body(): squares = squares + lax.ppermute(squares, 'tensor', swap_pairs(tensors))  1.59 us
    ppermute x1, waiting for transfers between devices, body(): far_squares = [lax.ppermute(squares, 'group', swap_pairs(groups))]  1.01 us
  transfers between devices with their start and end apart: 5, of which 2 were waited for; matrix products, arithmetic and copies ran while one was open for 7% of the time, Pallas kernels for 25%

profile of v6, /device:TPU:0, one launch (start us, length us, event | category | flops | bytes accessed | tf_op | source)
XLA Modules:
  0.0 45.6 jit_solution(10848621101921693203)
XLA Ops:
  0.0 0.0 copy-start
  0.0 0.0 copy-start.3
  0.0 0.0 copy-start.4
  0.0 0.0 copy-start.1
  0.0 0.0 copy-start.2
  0.0 0.5 %collective-permute-start.2 = (bf16[512,2560]{1,0:T(8,128)(2,1)}, bf16[512,2560]{1,0:T(8,128)(2,1)}, u32[]{:S(2)}, u32[]{:S(2)}) collective-permute-start(bf16[512,2560]{1,0:T(8,128)(2,1)} %refs_1_.1), channel_id=1, source_target_pairs={{0,2},{2,0},{4,6},{6,4},{8,10},{10,8},{12,14},{14,12},{16,18},{18,... | collective-permute-start | bytes 7864328 | tf_op jit(solution)/shard_map/ppermute | solution.py:352
  0.5 2.6 %multiply_reduce_fusion.1 = f32[512]{0:T(512)S(1)} fusion(bf16[512,2560]{1,0:T(8,128)(2,1)} %refs_1_.1), kind=kLoop, calls=%fused_computation.1 | loop fusion | flops 3931648 | bytes 2623488 | tf_op jit(solution)/shard_map/reduce_sum | solution.py:355
  3.2 0.0 copy-done
  3.2 0.6 %multiply_reduce_fusion = f32[512]{0:T(512)S(1)} fusion(bf16[512,2560]{1,0:T(8,128)(2,1)S(1)} %copy-done), kind=kLoop, calls=%fused_computation | loop fusion | flops 3931648 | bytes 2623488 | tf_op jit(solution)/shard_map/reduce_sum | solution.py:355
  3.8 2.4 %collective-permute-start = (f32[2,512]{1,0:T(2,128)S(1)}, f32[2,512]{1,0:T(2,128)S(1)}, u32[]{:S(2)}, u32[]{:S(2)}) collective-permute-start(f32[2,512]{1,0:T(2,128)S(1)} %pad_maximum_fusion), channel_id=1, source_target_pairs={{0,1},{1,0},{2,3},{3,2},{4,5},{5,4},{6,7},{7,6},{8,9},{9,8},{10,11... | collective-permute-start | bytes 12296 | tf_op jit(solution)/shard_map/ppermute | solution.py:357
  6.2 1.6 %collective-permute-done = f32[2,512]{1,0:T(2,128)S(1)} collective-permute-done((f32[2,512]{1,0:T(2,128)S(1)}, f32[2,512]{1,0:T(2,128)S(1)}, u32[]{:S(2)}, u32[]{:S(2)}) %collective-permute-start) | collective-permute-done | bytes 4128 | tf_op jit(solution)/shard_map/ppermute | solution.py:357
  7.8 0.1 collective-permute-start.1
  7.9 0.0 copy-done.3
  7.9 0.0 copy-done.4
  7.9 0.1 pad_add_fusion.facts_ref
  8.0 0.0 copy-done.1
  8.0 0.0 copy-done.2
  8.0 1.0 %collective-permute-done.1.refs_1_ = f32[2,512]{1,0:T(2,128)S(1)} collective-permute-done((f32[2,512]{1,0:T(2,128)S(1)}, f32[2,512]{1,0:T(2,128)S(1)}, u32[]{:S(2)}, u32[]{:S(2)}) %collective-permute-start.1) | collective-permute-done | bytes 4128 | tf_op jit(solution)/shard_map/ppermute | solution.py:361
  9.0 0.0 collective-permute-done.2.refs_3_
  9.0 19.4 %early_attention.1 = (bf16[512,2560]{1,0:T(8,128)(2,1)}, f32[512,128]{1,0:T(8,128)S(1)}, bf16[512,2560]{1,0:T(8,128)(2,1)}, f32[512,128]{1,0:T(8,128)S(1)}) custom-call(s32[33]{0:T(128)S(1)} %pad_add_fusion.facts_ref, f32[2,512]{1,0:T(2,128)S(1)} %fusion.refs_0_, f32[2,512]{1,0:T(2,128)S(1)} %collective-permute-done.1.refs_1_, bf16[512,2560]{1,0:T(8,128)(2,1)} %refs_1_.1, ...), custom_call_target="tpu_custom_call" | custom-call | flops 4026531840 | bytes 7864320 | tf_op jit(solution)/shard_map/early_attention/pallas_call | solution.py:396
  28.4 0.1 collective-permute-start.3
  28.5 0.5 %collective-permute-start.4 = (f32[512,128]{1,0:T(8,128)S(1)}, f32[512,128]{1,0:T(8,128)S(1)}, u32[]{:S(2)}, u32[]{:S(2)}) collective-permute-start(f32[512,128]{1,0:T(8,128)S(1)} %get-tuple-element.16), channel_id=1, source_target_pairs={{0,2},{2,0},{4,6},{6,4},{8,10},{10,8},{12,14},{14,12},{16,18},{18,... | collective-permute-start | bytes 786440 | tf_op jit(solution)/shard_map/ppermute | solution.py:406
  29.0 11.2 %late_attention.1 = (bf16[512,2560]{1,0:T(8,128)(2,1)}, f32[512,128]{1,0:T(8,128)S(1)}) custom-call(s32[33]{0:T(128)S(1)} %pad_add_fusion.facts_ref, f32[2,512]{1,0:T(2,128)S(1)} %fusion.refs_0_, bf16[512,2560]{1,0:T(8,128)(2,1)} %refs_1_.1, bf16[896,2560]{1,0:T(8,128)(2,1)} %refs_2_.3, ...), custom_call_target="tpu_custom_call", output_to_operand_aliasing={{0}: (9, {}), {1}: (10, {})} | custom-call | flops 4026531840 | bytes 7864320 | tf_op jit(solution)/shard_map/late_attention/pallas_call | solution.py:408
  40.2 0.0 collective-permute-done.4.far_stat
  40.2 0.0 collective-permute-done.3.far
  40.2 5.2 %join_parts.1 = bf16[512,2560]{1,0:T(8,128)(2,1)} custom-call(s32[33]{0:T(128)S(1)} %pad_add_fusion.facts_ref, bf16[512,2560]{1,0:T(8,128)(2,1)} %get-tuple-element.13.own_any, f32[512,128]{1,0:T(8,128)S(1)} %get-tuple-element.14.stat, bf16[512,2560]{1,0:T(8,128)(2,1)S(1)} %collective-permute-done.3.far, ...), custom_call_target="tpu_custom_call", output_to_operand_aliasing={{}: (1, {})} | custom-call | tf_op jit(solution)/shard_map/join_parts/pallas_call | solution.py:422
  (4 shorter events, 0.0 us)
Async XLA Ops:
  0.0 3.2 %copy-start = (bf16[512,2560]{1,0:T(8,128)(2,1)S(1)}, bf16[512,2560]{1,0:T(8,128)(2,1)}, u32[]{:S(2)}) copy-start(bf16[512,2560]{1,0:T(8,128)(2,1)} %refs_4_.3) | copy-start | bytes 7864324
  0.0 7.9 %copy-start.3 = (s32[16]{0:T(128)S(1)}, s32[16]{0:T(128)}, u32[]{:S(2)}) copy-start(s32[16]{0:T(128)} %param.17) | copy-start | bytes 196
  0.0 7.9 %copy-start.4 = (s32[16]{0:T(128)S(1)}, s32[16]{0:T(128)}, u32[]{:S(2)}) copy-start(s32[16]{0:T(128)} %param.16) | copy-start | bytes 196
  0.0 8.0 %copy-start.1 = (f32[2560]{0:T(1024)S(1)}, f32[2560]{0:T(1024)}, u32[]{:S(2)}) copy-start(f32[2560]{0:T(1024)} %param.14) | copy-start | bytes 30724
  0.0 8.0 %copy-start.2 = (f32[2560]{0:T(1024)S(1)}, f32[2560]{0:T(1024)}, u32[]{:S(2)}) copy-start(f32[2560]{0:T(1024)} %param.15) | copy-start | bytes 30724
  0.0 9.0 %collective-permute-start.2 = (bf16[512,2560]{1,0:T(8,128)(2,1)}, bf16[512,2560]{1,0:T(8,128)(2,1)}, u32[]{:S(2)}, u32[]{:S(2)}) collective-permute-start(bf16[512,2560]{1,0:T(8,128)(2,1)} %refs_1_.1), channel_id=1, source_target_pairs={{0,2},{2,0},{4,6},{6,4},{8,10},{10,8},{12,14},{14,12},{16,18},{18,... | collective-permute-start | bytes 7864328 | tf_op jit(solution)/shard_map/ppermute | solution.py:352
  3.8 4.0 %collective-permute-start = (f32[2,512]{1,0:T(2,128)S(1)}, f32[2,512]{1,0:T(2,128)S(1)}, u32[]{:S(2)}, u32[]{:S(2)}) collective-permute-start(f32[2,512]{1,0:T(2,128)S(1)} %pad_maximum_fusion), channel_id=1, source_target_pairs={{0,1},{1,0},{2,3},{3,2},{4,5},{5,4},{6,7},{7,6},{8,9},{9,8},{10,11... | collective-permute-start | bytes 12296 | tf_op jit(solution)/shard_map/ppermute | solution.py:357
  7.8 1.2 %collective-permute-start.1 = (f32[2,512]{1,0:T(2,128)S(1)}, f32[2,512]{1,0:T(2,128)S(1)}, u32[]{:S(2)}, u32[]{:S(2)}) collective-permute-start(f32[2,512]{1,0:T(2,128)S(1)} %fusion.refs_0_), channel_id=1, source_target_pairs={{0,2},{2,0},{4,6},{6,4},{8,10},{10,8},{12,14},{14,12},{16,18},{18,... | collective-permute-start | bytes 12296 | tf_op jit(solution)/shard_map/ppermute | solution.py:361
  28.4 11.8 %collective-permute-start.3 = (bf16[512,2560]{1,0:T(8,128)(2,1)}, bf16[512,2560]{1,0:T(8,128)(2,1)S(1)}, u32[]{:S(2)}, u32[]{:S(2)}) collective-permute-start(bf16[512,2560]{1,0:T(8,128)(2,1)} %get-tuple-element.15), channel_id=1, source_target_pairs={{0,2},{2,0},{4,6},{6,4},{8,10},{10,8},{12,14},{14,12},{16,18},{18,... | collective-permute-start | bytes 7864328 | tf_op jit(solution)/shard_map/ppermute | solution.py:406
  28.5 11.7 %collective-permute-start.4 = (f32[512,128]{1,0:T(8,128)S(1)}, f32[512,128]{1,0:T(8,128)S(1)}, u32[]{:S(2)}, u32[]{:S(2)}) collective-permute-start(f32[512,128]{1,0:T(8,128)S(1)} %get-tuple-element.16), channel_id=1, source_target_pairs={{0,2},{2,0},{4,6},{6,4},{8,10},{10,8},{12,14},{14,12},{16,18},{18,... | collective-permute-start | bytes 786440 | tf_op jit(solution)/shard_map/ppermute | solution.py:406

commit v7 on v4

--- a/solution.py
+++ b/solution.py
@@ -72,7 +72,7 @@
         self.q, self.q_scale, self.q_gain = q, q_scale, q_gain
         self.keys, self.values, self.tail, self.fresh = keys, values, tail, fresh
         self.out, self.stat = out, stat
-        self.scores, self.tops, self.weights = scratch
+        self.scores, self.tops, self.weights, self.sums = scratch
         self.rows = q.shape[0]
         self.cached = keys.shape[0]
         self.total = self.cached + (fresh[0].shape[0] if fresh else 0)
@@ -102,23 +102,26 @@
 
     def soften(self, head, slot):
         top = self.tops[slot][...]
+        total = None
         for start in range(0, self.total, CB):
-            column = self.scores[slot][:, start : start + CB]
-            self.weights[slot][:, start : start + CB] = jnp.exp2(column - top).astype(jnp.bfloat16)
+            weights = jnp.exp2(self.scores[slot][:, start : start + CB] - top)
+            self.weights[slot][:, start : start + CB] = weights.astype(jnp.bfloat16)
+            total = weights if total is None else total + weights
+        total = jnp.broadcast_to(jnp.sum(total, axis=1, keepdims=True), (self.rows, HD))
+        self.sums[slot][...] = total
         pltpu.store(self.stat, top, mask=self.lane == head)
-
-    def mix(self, head, target, lane, slot):
+        pltpu.store(self.stat, total, mask=self.lane == head + SUM_LANE)
+
+    def mix(self, head, target, slot):
         cut = lanes(head)
         values = self.values[:, cut]
         if self.fresh:
             values = jnp.concatenate([values, self.fresh[1][:, cut]], axis=0)
-        wide = jnp.concatenate([values, jnp.ones_like(values)], axis=1)
-        mixture = jnp.dot(self.weights[slot][:, : self.total], wide, preferred_element_type=jnp.float32)
-        totals = mixture[:, HD:]
+        mixture = jnp.dot(self.weights[slot][:, : self.total], values, preferred_element_type=jnp.float32)
+        totals = self.sums[slot][...]
         inverse = pl.reciprocal(totals, approx=True)
         inverse = inverse * (2.0 - totals * inverse)
-        self.out[:, lanes(target)] = (mixture[:, :HD] * inverse).astype(jnp.bfloat16)
-        pltpu.store(self.stat, totals, mask=self.lane == lane + SUM_LANE)
+        self.out[:, lanes(target)] = (mixture * inverse).astype(jnp.bfloat16)
 
     def run(self, first, last, spare, ready, done, finish=None):
         ready(first, True)
@@ -136,10 +139,10 @@
             ready(head + 2, False)
             self.score(second, 1)
             self.soften(head, 0)
-            self.mix(before, jnp.where(begun, before, spare), jnp.where(begun, before, SUM_LANE - 1), 1)
+            self.mix(before, jnp.where(begun, before, spare), 1)
             self.score(later, 0)
             self.soften(second, 1)
-            self.mix(head, head, head, 0)
+            self.mix(head, head, 0)
             done(head).start()
 
             @pl.when(begun)
@@ -149,7 +152,7 @@
             return carry
 
         lax.fori_loop(0, lax.shift_right_logical(count + 1, 1), step, 0)
-        self.mix(last - 1, jnp.where(paired, last - 1, spare), last - 1, 1)
+        self.mix(last - 1, jnp.where(paired, last - 1, spare), 1)
 
         @pl.when(paired)
         def _():
@@ -202,10 +205,10 @@
 def early_kernel(facts_ref, *refs, slots, heads, chunk, sums):
     own_squares, far_squares, refs = refs[:sums], refs[sums : 2 * sums], refs[2 * sums :]
     (q_any, far_q_any, k_any, v_any, nk_any, nv_any, qg, kg, far_any, far_stat_any, own_any, stat_any) = refs[:12]
-    q, k, v, nk, nv, out, stat, q_scale, k_scale, s0, s1, t0, t1, w0, w1, in_sems, out_sems, stat_sem = refs[12:]
+    q, k, v, nk, nv, out, stat, q_scale, k_scale, s0, s1, t0, t1, w0, w1, u0, u1, in_sems, out_sems, stat_sem = refs[12:]
     own_home, own_tail, held, far_tail, away = counts(facts_ref, slots)
     fresh_rows = nk.shape[0]
-    scratch = ((s0, s1), (t0, t1), (w0, w1))
+    scratch = ((s0, s1), (t0, t1), (w0, w1), (u0, u1))
 
     def writer(target):
         def copy(head):
@@ -254,10 +257,10 @@
 def late_kernel(facts_ref, *refs, slots, heads, chunk, sums):
     own_squares, refs = refs[:sums], refs[sums:]
     (q_any, k_any, v_any, nk_any, nv_any, qg, kg, _, _, own_any, stat_any) = refs[:11]
-    q, k, v, nk, nv, out, stat, q_scale, k_scale, s0, s1, t0, t1, w0, w1, in_sems, out_sems, stat_sem = refs[11:]
+    q, k, v, nk, nv, out, stat, q_scale, k_scale, s0, s1, t0, t1, w0, w1, u0, u1, in_sems, out_sems, stat_sem = refs[11:]
     own_home, own_tail, held, far_tail, away = counts(facts_ref, slots)
     fresh_rows = nk.shape[0]
-    scratch = ((s0, s1), (t0, t1), (w0, w1))
+    scratch = ((s0, s1), (t0, t1), (w0, w1), (u0, u1))
     first = early_heads(away, heads, slots, fresh_rows // CB)
 
     def own_scale():
@@ -374,6 +377,7 @@
         pltpu.VMEM((half, keys), jnp.float32), pltpu.VMEM((half, keys), jnp.float32),
         pltpu.VMEM((half, HD), jnp.float32), pltpu.VMEM((half, HD), jnp.float32),
         pltpu.VMEM((half, keys), jnp.bfloat16), pltpu.VMEM((half, keys), jnp.bfloat16),
+        stat_space, stat_space,
         pltpu.SemaphoreType.DMA((5, heads // chunk)), pltpu.SemaphoreType.DMA((heads,)), pltpu.SemaphoreType.DMA,
     ]
     pairs = row_count * heads * CB

time: 44.8 us -> 49 us (1.094)
  the two profiles are of different devices: /device:TPU:0 before, /device:TPU:7 now
where the time goes in v7:
time: 49 us; the launch traced here: 48.6 us
  Pallas kernels  39.3 us (80%)
  other arithmetic  3.09 us (6%)
  starting transfers between devices  2.93 us (6%)
  waiting for transfers between devices  2.91 us (6%)
    pallas_call x1, Pallas kernels, body(): pl.pallas_call(functools.partial(late_kernel, slots=slots, heads=heads, c...  19.6 us
    pallas_call x1, Pallas kernels, body(): pl.pallas_call(functools.partial(early_kernel, slots=slots, heads=heads,...  14.5 us
    pallas_call x1, Pallas kernels, body(): pl.pallas_call(functools.partial(join_kernel, slots=slots, step_rows=step...  5.19 us
    reduce_sum x1, other arithmetic, body(): jnp.sum(wide_q * wide_q, axis=1)  2.41 us
    ppermute x1, waiting for transfers between devices, body(): squares = squares + lax.ppermute(squares, 'tensor', swap_pairs(tensors))  2.2 us
    ppermute x1, starting transfers between devices, body(): far_squares = [lax.ppermute(squares, 'group', swap_pairs(groups))]  1.29 us
  transfers between devices with their start and end apart: 5, of which 2 were waited for; matrix products, arithmetic and copies ran while one was open for 6% of the time, Pallas kernels for 40%

profile of v7, /device:TPU:7, one launch (start us, length us, event | category | flops | bytes accessed | tf_op | source)
XLA Modules:
  0.0 48.6 jit_solution(17607175316690508656)
XLA Ops:
  0.0 0.0 copy-start
  0.0 0.0 copy-start.3
  0.0 0.0 copy-start.4
  0.0 0.0 copy-start.1
  0.0 0.0 copy-start.2
  0.0 0.7 %collective-permute-start.2 = (bf16[512,2560]{1,0:T(8,128)(2,1)}, bf16[512,2560]{1,0:T(8,128)(2,1)}, u32[]{:S(2)}, u32[]{:S(2)}) collective-permute-start(bf16[512,2560]{1,0:T(8,128)(2,1)} %refs_1_.1), channel_id=1, source_target_pairs={{0,2},{2,0},{4,6},{6,4},{8,10},{10,8},{12,14},{14,12},{16,18},{18,... | collective-permute-start | bytes 7864328 | tf_op jit(solution)/shard_map/ppermute | solution.py:348
  0.8 2.4 %multiply_reduce_fusion.1 = f32[512]{0:T(512)S(1)} fusion(bf16[512,2560]{1,0:T(8,128)(2,1)} %refs_1_.1), kind=kLoop, calls=%fused_computation.1 | loop fusion | flops 3931648 | bytes 2623488 | tf_op jit(solution)/shard_map/reduce_sum | solution.py:351
  3.2 0.0 copy-done
  3.2 0.6 %multiply_reduce_fusion = f32[512]{0:T(512)S(1)} fusion(bf16[512,2560]{1,0:T(8,128)(2,1)S(1)} %copy-done), kind=kLoop, calls=%fused_computation | loop fusion | flops 3931648 | bytes 2623488 | tf_op jit(solution)/shard_map/reduce_sum | solution.py:351
  3.8 0.3 collective-permute-start
  4.1 2.2 %collective-permute-done = f32[2,512]{1,0:T(2,128)S(1)} collective-permute-done((f32[2,512]{1,0:T(2,128)S(1)}, f32[2,512]{1,0:T(2,128)S(1)}, u32[]{:S(2)}, u32[]{:S(2)}) %collective-permute-start) | collective-permute-done | bytes 4128 | tf_op jit(solution)/shard_map/ppermute | solution.py:353
  6.3 1.3 %collective-permute-start.1 = (f32[2,512]{1,0:T(2,128)S(1)}, f32[2,512]{1,0:T(2,128)S(1)}, u32[]{:S(2)}, u32[]{:S(2)}) collective-permute-start(f32[2,512]{1,0:T(2,128)S(1)} %fusion.refs_0_), channel_id=1, source_target_pairs={{0,2},{2,0},{4,6},{6,4},{8,10},{10,8},{12,14},{14,12},{16,18},{18,... | collective-permute-start | bytes 12296 | tf_op jit(solution)/shard_map/ppermute | solution.py:357
  7.6 0.0 copy-done.3
  7.6 0.0 copy-done.4
  7.6 0.1 pad_add_fusion.facts_ref
  7.7 0.0 copy-done.1
  7.7 0.0 copy-done.2
  7.7 0.7 %collective-permute-done.1.refs_1_ = f32[2,512]{1,0:T(2,128)S(1)} collective-permute-done((f32[2,512]{1,0:T(2,128)S(1)}, f32[2,512]{1,0:T(2,128)S(1)}, u32[]{:S(2)}, u32[]{:S(2)}) %collective-permute-start.1) | collective-permute-done | bytes 4128 | tf_op jit(solution)/shard_map/ppermute | solution.py:357
  8.4 0.0 collective-permute-done.2.refs_3_
  8.4 14.5 %early_attention.1 = (bf16[512,2560]{1,0:T(8,128)(2,1)}, f32[512,128]{1,0:T(8,128)S(1)}, bf16[512,2560]{1,0:T(8,128)(2,1)}, f32[512,128]{1,0:T(8,128)S(1)}) custom-call(s32[33]{0:T(128)S(1)} %pad_add_fusion.facts_ref, f32[2,512]{1,0:T(2,128)S(1)} %fusion.refs_0_, f32[2,512]{1,0:T(2,128)S(1)} %collective-permute-done.1.refs_1_, bf16[512,2560]{1,0:T(8,128)(2,1)} %refs_1_.1, ...), custom_call_target="tpu_custom_call" | custom-call | flops 4026531840 | bytes 7864320 | tf_op jit(solution)/shard_map/early_attention/pallas_call | solution.py:393
  23.0 0.1 collective-permute-start.3
  23.1 0.5 %collective-permute-start.4 = (f32[512,128]{1,0:T(8,128)S(1)}, f32[512,128]{1,0:T(8,128)S(1)}, u32[]{:S(2)}, u32[]{:S(2)}) collective-permute-start(f32[512,128]{1,0:T(8,128)S(1)} %get-tuple-element.16), channel_id=1, source_target_pairs={{0,2},{2,0},{4,6},{6,4},{8,10},{10,8},{12,14},{14,12},{16,18},{18,... | collective-permute-start | bytes 786440 | tf_op jit(solution)/shard_map/ppermute | solution.py:403
  23.6 19.6 %late_attention.1 = (bf16[512,2560]{1,0:T(8,128)(2,1)}, f32[512,128]{1,0:T(8,128)S(1)}) custom-call(s32[33]{0:T(128)S(1)} %pad_add_fusion.facts_ref, f32[2,512]{1,0:T(2,128)S(1)} %fusion.refs_0_, bf16[512,2560]{1,0:T(8,128)(2,1)} %refs_1_.1, bf16[896,2560]{1,0:T(8,128)(2,1)} %refs_2_.3, ...), custom_call_target="tpu_custom_call", output_to_operand_aliasing={{0}: (9, {}), {1}: (10, {})} | custom-call | flops 4026531840 | bytes 7864320 | tf_op jit(solution)/shard_map/late_attention/pallas_call | solution.py:405
  43.2 0.0 collective-permute-done.4.far_stat
  43.2 0.0 collective-permute-done.3.far
  43.2 5.2 %join_parts.1 = bf16[512,2560]{1,0:T(8,128)(2,1)} custom-call(s32[33]{0:T(128)S(1)} %pad_add_fusion.facts_ref, bf16[512,2560]{1,0:T(8,128)(2,1)} %get-tuple-element.13.own_any, f32[512,128]{1,0:T(8,128)S(1)} %get-tuple-element.14.stat, bf16[512,2560]{1,0:T(8,128)(2,1)S(1)} %collective-permute-done.3.far, ...), custom_call_target="tpu_custom_call", output_to_operand_aliasing={{}: (1, {})} | custom-call | tf_op jit(solution)/shard_map/join_parts/pallas_call | solution.py:419
  (4 shorter events, 0.0 us)
Async XLA Ops:
  0.0 3.2 %copy-start = (bf16[512,2560]{1,0:T(8,128)(2,1)S(1)}, bf16[512,2560]{1,0:T(8,128)(2,1)}, u32[]{:S(2)}) copy-start(bf16[512,2560]{1,0:T(8,128)(2,1)} %refs_4_.3) | copy-start | bytes 7864324
  0.0 7.6 %copy-start.3 = (s32[16]{0:T(128)S(1)}, s32[16]{0:T(128)}, u32[]{:S(2)}) copy-start(s32[16]{0:T(128)} %param.17) | copy-start | bytes 196
  0.0 7.6 %copy-start.4 = (s32[16]{0:T(128)S(1)}, s32[16]{0:T(128)}, u32[]{:S(2)}) copy-start(s32[16]{0:T(128)} %param.16) | copy-start | bytes 196
  0.0 7.7 %copy-start.1 = (f32[2560]{0:T(1024)S(1)}, f32[2560]{0:T(1024)}, u32[]{:S(2)}) copy-start(f32[2560]{0:T(1024)} %param.14) | copy-start | bytes 30724
  0.0 7.7 %copy-start.2 = (f32[2560]{0:T(1024)S(1)}, f32[2560]{0:T(1024)}, u32[]{:S(2)}) copy-start(f32[2560]{0:T(1024)} %param.15) | copy-start | bytes 30724
  0.0 8.4 %collective-permute-start.2 = (bf16[512,2560]{1,0:T(8,128)(2,1)}, bf16[512,2560]{1,0:T(8,128)(2,1)}, u32[]{:S(2)}, u32[]{:S(2)}) collective-permute-start(bf16[512,2560]{1,0:T(8,128)(2,1)} %refs_1_.1), channel_id=1, source_target_pairs={{0,2},{2,0},{4,6},{6,4},{8,10},{10,8},{12,14},{14,12},{16,18},{18,... | collective-permute-start | bytes 7864328 | tf_op jit(solution)/shard_map/ppermute | solution.py:348
  3.8 2.5 %collective-permute-start = (f32[2,512]{1,0:T(2,128)S(1)}, f32[2,512]{1,0:T(2,128)S(1)}, u32[]{:S(2)}, u32[]{:S(2)}) collective-permute-start(f32[2,512]{1,0:T(2,128)S(1)} %pad_maximum_fusion), channel_id=1, source_target_pairs={{0,1},{1,0},{2,3},{3,2},{4,5},{5,4},{6,7},{7,6},{8,9},{9,8},{10,11... | collective-permute-start | bytes 12296 | tf_op jit(solution)/shard_map/ppermute | solution.py:353
  6.3 2.1 %collective-permute-start.1 = (f32[2,512]{1,0:T(2,128)S(1)}, f32[2,512]{1,0:T(2,128)S(1)}, u32[]{:S(2)}, u32[]{:S(2)}) collective-permute-start(f32[2,512]{1,0:T(2,128)S(1)} %fusion.refs_0_), channel_id=1, source_target_pairs={{0,2},{2,0},{4,6},{6,4},{8,10},{10,8},{12,14},{14,12},{16,18},{18,... | collective-permute-start | bytes 12296 | tf_op jit(solution)/shard_map/ppermute | solution.py:357
  23.0 20.2 %collective-permute-start.3 = (bf16[512,2560]{1,0:T(8,128)(2,1)}, bf16[512,2560]{1,0:T(8,128)(2,1)S(1)}, u32[]{:S(2)}, u32[]{:S(2)}) collective-permute-start(bf16[512,2560]{1,0:T(8,128)(2,1)} %get-tuple-element.15), channel_id=1, source_target_pairs={{0,2},{2,0},{4,6},{6,4},{8,10},{10,8},{12,14},{14,12},{16,18},{18,... | collective-permute-start | bytes 7864328 | tf_op jit(solution)/shard_map/ppermute | solution.py:403
  23.1 20.1 %collective-permute-start.4 = (f32[512,128]{1,0:T(8,128)S(1)}, f32[512,128]{1,0:T(8,128)S(1)}, u32[]{:S(2)}, u32[]{:S(2)}) collective-permute-start(f32[512,128]{1,0:T(8,128)S(1)} %get-tuple-element.16), channel_id=1, source_target_pairs={{0,2},{2,0},{4,6},{6,4},{8,10},{10,8},{12,14},{14,12},{16,18},{18,... | collective-permute-start | bytes 786440 | tf_op jit(solution)/shard_map/ppermute | solution.py:403

commit v8 on v4

--- a/solution.py
+++ b/solution.py
@@ -16,7 +16,8 @@
 SCALE = math.log2(math.e) / math.sqrt(HD)
 SUM_LANE = 64
 VMEM = 53 * 1024 * 1024
-KEYS = 256
+KEYS = 512
+PIECE = 64
 
 
 def swap_pairs(count):
@@ -87,18 +88,25 @@
             new_k, _, k_scale, k_gain = self.fresh
             raw_k = new_k[:, cut].astype(jnp.float32)
             keys = jnp.concatenate([keys, (raw_k * k_scale[...] * k_gain[:, cut]).astype(jnp.bfloat16)], axis=0)
-        top = None
+        tops = [None] * (self.rows // PIECE)
+        lane = self.lane[:PIECE]
         for begin in range(0, self.total, KEYS):
             scores = lax.dot_general(
                 queries, keys[begin : begin + KEYS], (((1,), (1,)), ((), ())), preferred_element_type=jnp.float32
             )
-            for start in range(begin, min(begin + KEYS, self.total), CB):
-                column = scores[:, start - begin : start - begin + CB]
-                if start == self.cached - CB:
-                    column = jnp.where(self.lane < self.tail, column, NEGATIVE)
-                self.scores[slot][:, start : start + CB] = column
-                top = column if top is None else jnp.maximum(top, column)
-        self.tops[slot][...] = jnp.broadcast_to(jnp.max(top, axis=1, keepdims=True), (self.rows, HD))
+            for index in range(len(tops)):
+                piece = slice(index * PIECE, (index + 1) * PIECE)
+                top = tops[index]
+                for start in range(begin, min(begin + KEYS, self.total), CB):
+                    column = scores[piece, start - begin : start - begin + CB]
+                    if start == self.cached - CB:
+                        column = jnp.where(lane < self.tail, column, NEGATIVE)
+                    self.scores[slot][piece, start : start + CB] = column
+                    top = column if top is None else jnp.maximum(top, column)
+                tops[index] = top
+        for index, top in enumerate(tops):
+            piece = slice(index * PIECE, (index + 1) * PIECE)
+            self.tops[slot][piece, :] = jnp.broadcast_to(jnp.max(top, axis=1, keepdims=True), (PIECE, HD))
 
     def soften(self, head, slot):
         top = self.tops[slot][...]

time: 44.8 us -> 44.8 us (level)
  the two profiles are of different devices: /device:TPU:0 before, /device:TPU:1 now
where the time goes in v8:
time: 44.8 us; the launch traced here: 44.5 us
  Pallas kernels  34.9 us (78%)
  starting transfers between devices  4.38 us (10%)
  other arithmetic  3.16 us (7%)
  waiting for transfers between devices  1.69 us (4%)
    pallas_call x1, Pallas kernels, body(): pl.pallas_call(functools.partial(late_kernel, slots=slots, heads=heads, c...  17 us
    pallas_call x1, Pallas kernels, body(): pl.pallas_call(functools.partial(early_kernel, slots=slots, heads=heads,...  12.7 us
    pallas_call x1, Pallas kernels, body(): pl.pallas_call(functools.partial(join_kernel, slots=slots, step_rows=step...  5.19 us
    ppermute x1, starting transfers between devices, body(): squares = squares + lax.ppermute(squares, 'tensor', swap_pairs(tensors))  2.68 us
    reduce_sum x1, other arithmetic, body(): jnp.sum(wide_q * wide_q, axis=1)  2.48 us
    ppermute x1, starting transfers between devices, body(): far_squares = [lax.ppermute(squares, 'group', swap_pairs(groups))]  1.02 us
    ppermute x1, waiting for transfers between devices, body(): squares = squares + lax.ppermute(squares, 'tensor', swap_pairs(tensors))  0.98 us
  transfers between devices with their start and end apart: 5, of which 2 were waited for; matrix products, arithmetic and copies ran while one was open for 7% of the time, Pallas kernels for 38%

profile of v8, /device:TPU:1, one launch (start us, length us, event | category | flops | bytes accessed | tf_op | source)
XLA Modules:
  0.0 44.5 jit_solution(10903515310816711379)
XLA Ops:
  0.0 0.0 copy-start
  0.0 0.0 copy-start.3
  0.0 0.0 copy-start.4
  0.0 0.0 copy-start.1
  0.0 0.0 copy-start.2
  0.0 0.1 collective-permute-start.2
  0.1 2.5 %multiply_reduce_fusion.1 = f32[512]{0:T(512)S(1)} fusion(bf16[512,2560]{1,0:T(8,128)(2,1)} %refs_1_.1), kind=kLoop, calls=%fused_computation.1 | loop fusion | flops 3931648 | bytes 2623488 | tf_op jit(solution)/shard_map/reduce_sum | solution.py:356
  2.6 0.0 copy-done
  2.6 0.6 %multiply_reduce_fusion = f32[512]{0:T(512)S(1)} fusion(bf16[512,2560]{1,0:T(8,128)(2,1)S(1)} %copy-done), kind=kLoop, calls=%fused_computation | loop fusion | flops 3931648 | bytes 2623488 | tf_op jit(solution)/shard_map/reduce_sum | solution.py:356
  3.2 2.7 %collective-permute-start = (f32[2,512]{1,0:T(2,128)S(1)}, f32[2,512]{1,0:T(2,128)S(1)}, u32[]{:S(2)}, u32[]{:S(2)}) collective-permute-start(f32[2,512]{1,0:T(2,128)S(1)} %pad_maximum_fusion), channel_id=1, source_target_pairs={{0,1},{1,0},{2,3},{3,2},{4,5},{5,4},{6,7},{7,6},{8,9},{9,8},{10,11... | collective-permute-start | bytes 12296 | tf_op jit(solution)/shard_map/ppermute | solution.py:358
  5.9 1.0 %collective-permute-done = f32[2,512]{1,0:T(2,128)S(1)} collective-permute-done((f32[2,512]{1,0:T(2,128)S(1)}, f32[2,512]{1,0:T(2,128)S(1)}, u32[]{:S(2)}, u32[]{:S(2)}) %collective-permute-start) | collective-permute-done | bytes 4128 | tf_op jit(solution)/shard_map/ppermute | solution.py:358
  6.9 1.0 %collective-permute-start.1 = (f32[2,512]{1,0:T(2,128)S(1)}, f32[2,512]{1,0:T(2,128)S(1)}, u32[]{:S(2)}, u32[]{:S(2)}) collective-permute-start(f32[2,512]{1,0:T(2,128)S(1)} %fusion.refs_0_), channel_id=1, source_target_pairs={{0,2},{2,0},{4,6},{6,4},{8,10},{10,8},{12,14},{14,12},{16,18},{18,... | collective-permute-start | bytes 12296 | tf_op jit(solution)/shard_map/ppermute | solution.py:362
  7.9 0.0 copy-done.3
  7.9 0.0 copy-done.4
  7.9 0.1 pad_add_fusion.facts_ref
  8.0 0.0 copy-done.1
  8.0 0.0 copy-done.2
  8.0 0.7 %collective-permute-done.1.refs_1_ = f32[2,512]{1,0:T(2,128)S(1)} collective-permute-done((f32[2,512]{1,0:T(2,128)S(1)}, f32[2,512]{1,0:T(2,128)S(1)}, u32[]{:S(2)}, u32[]{:S(2)}) %collective-permute-start.1) | collective-permute-done | bytes 4128 | tf_op jit(solution)/shard_map/ppermute | solution.py:362
  8.7 0.0 collective-permute-done.2.refs_3_
  8.7 12.7 %early_attention.1 = (bf16[512,2560]{1,0:T(8,128)(2,1)}, f32[512,128]{1,0:T(8,128)S(1)}, bf16[512,2560]{1,0:T(8,128)(2,1)}, f32[512,128]{1,0:T(8,128)S(1)}) custom-call(s32[33]{0:T(128)S(1)} %pad_add_fusion.facts_ref, f32[2,512]{1,0:T(2,128)S(1)} %fusion.refs_0_, f32[2,512]{1,0:T(2,128)S(1)} %collective-permute-done.1.refs_1_, bf16[512,2560]{1,0:T(8,128)(2,1)} %refs_1_.1, ...), custom_call_target="tpu_custom_call" | custom-call | flops 4026531840 | bytes 7864320 | tf_op jit(solution)/shard_map/early_attention/pallas_call | solution.py:397
  21.4 0.1 collective-permute-start.3
  21.5 0.5 %collective-permute-start.4 = (f32[512,128]{1,0:T(8,128)S(1)}, f32[512,128]{1,0:T(8,128)S(1)}, u32[]{:S(2)}, u32[]{:S(2)}) collective-permute-start(f32[512,128]{1,0:T(8,128)S(1)} %get-tuple-element.16), channel_id=1, source_target_pairs={{0,2},{2,0},{4,6},{6,4},{8,10},{10,8},{12,14},{14,12},{16,18},{18,... | collective-permute-start | bytes 786440 | tf_op jit(solution)/shard_map/ppermute | solution.py:407
  22.0 17.0 %late_attention.1 = (bf16[512,2560]{1,0:T(8,128)(2,1)}, f32[512,128]{1,0:T(8,128)S(1)}) custom-call(s32[33]{0:T(128)S(1)} %pad_add_fusion.facts_ref, f32[2,512]{1,0:T(2,128)S(1)} %fusion.refs_0_, bf16[512,2560]{1,0:T(8,128)(2,1)} %refs_1_.1, bf16[896,2560]{1,0:T(8,128)(2,1)} %refs_2_.3, ...), custom_call_target="tpu_custom_call", output_to_operand_aliasing={{0}: (9, {}), {1}: (10, {})} | custom-call | flops 4026531840 | bytes 7864320 | tf_op jit(solution)/shard_map/late_attention/pallas_call | solution.py:409
  39.1 0.0 collective-permute-done.4.far_stat
  39.1 0.0 collective-permute-done.3.far
  39.1 5.2 %join_parts.1 = bf16[512,2560]{1,0:T(8,128)(2,1)} custom-call(s32[33]{0:T(128)S(1)} %pad_add_fusion.facts_ref, bf16[512,2560]{1,0:T(8,128)(2,1)} %get-tuple-element.13.own_any, f32[512,128]{1,0:T(8,128)S(1)} %get-tuple-element.14.stat, bf16[512,2560]{1,0:T(8,128)(2,1)S(1)} %collective-permute-done.3.far, ...), custom_call_target="tpu_custom_call", output_to_operand_aliasing={{}: (1, {})} | custom-call | tf_op jit(solution)/shard_map/join_parts/pallas_call | solution.py:423
  (4 shorter events, 0.0 us)
Async XLA Ops:
  0.0 2.6 %copy-start = (bf16[512,2560]{1,0:T(8,128)(2,1)S(1)}, bf16[512,2560]{1,0:T(8,128)(2,1)}, u32[]{:S(2)}) copy-start(bf16[512,2560]{1,0:T(8,128)(2,1)} %refs_4_.3) | copy-start | bytes 7864324
  0.0 7.9 %copy-start.3 = (s32[16]{0:T(128)S(1)}, s32[16]{0:T(128)}, u32[]{:S(2)}) copy-start(s32[16]{0:T(128)} %param.17) | copy-start | bytes 196
  0.0 7.9 %copy-start.4 = (s32[16]{0:T(128)S(1)}, s32[16]{0:T(128)}, u32[]{:S(2)}) copy-start(s32[16]{0:T(128)} %param.16) | copy-start | bytes 196
  0.0 8.0 %copy-start.1 = (f32[2560]{0:T(1024)S(1)}, f32[2560]{0:T(1024)}, u32[]{:S(2)}) copy-start(f32[2560]{0:T(1024)} %param.14) | copy-start | bytes 30724
  0.0 8.0 %copy-start.2 = (f32[2560]{0:T(1024)S(1)}, f32[2560]{0:T(1024)}, u32[]{:S(2)}) copy-start(f32[2560]{0:T(1024)} %param.15) | copy-start | bytes 30724
  0.0 8.7 %collective-permute-start.2 = (bf16[512,2560]{1,0:T(8,128)(2,1)}, bf16[512,2560]{1,0:T(8,128)(2,1)}, u32[]{:S(2)}, u32[]{:S(2)}) collective-permute-start(bf16[512,2560]{1,0:T(8,128)(2,1)} %refs_1_.1), channel_id=1, source_target_pairs={{0,2},{2,0},{4,6},{6,4},{8,10},{10,8},{12,14},{14,12},{16,18},{18,... | collective-permute-start | bytes 7864328 | tf_op jit(solution)/shard_map/ppermute | solution.py:353
  3.2 3.7 %collective-permute-start = (f32[2,512]{1,0:T(2,128)S(1)}, f32[2,512]{1,0:T(2,128)S(1)}, u32[]{:S(2)}, u32[]{:S(2)}) collective-permute-start(f32[2,512]{1,0:T(2,128)S(1)} %pad_maximum_fusion), channel_id=1, source_target_pairs={{0,1},{1,0},{2,3},{3,2},{4,5},{5,4},{6,7},{7,6},{8,9},{9,8},{10,11... | collective-permute-start | bytes 12296 | tf_op jit(solution)/shard_map/ppermute | solution.py:358
  6.9 1.8 %collective-permute-start.1 = (f32[2,512]{1,0:T(2,128)S(1)}, f32[2,512]{1,0:T(2,128)S(1)}, u32[]{:S(2)}, u32[]{:S(2)}) collective-permute-start(f32[2,512]{1,0:T(2,128)S(1)} %fusion.refs_0_), channel_id=1, source_target_pairs={{0,2},{2,0},{4,6},{6,4},{8,10},{10,8},{12,14},{14,12},{16,18},{18,... | collective-permute-start | bytes 12296 | tf_op jit(solution)/shard_map/ppermute | solution.py:362
  21.4 17.6 %collective-permute-start.3 = (bf16[512,2560]{1,0:T(8,128)(2,1)}, bf16[512,2560]{1,0:T(8,128)(2,1)S(1)}, u32[]{:S(2)}, u32[]{:S(2)}) collective-permute-start(bf16[512,2560]{1,0:T(8,128)(2,1)} %get-tuple-element.15), channel_id=1, source_target_pairs={{0,2},{2,0},{4,6},{6,4},{8,10},{10,8},{12,14},{14,12},{16,18},{18,... | collective-permute-start | bytes 7864328 | tf_op jit(solution)/shard_map/ppermute | solution.py:407
  21.5 17.5 %collective-permute-start.4 = (f32[512,128]{1,0:T(8,128)S(1)}, f32[512,128]{1,0:T(8,128)S(1)}, u32[]{:S(2)}, u32[]{:S(2)}) collective-permute-start(f32[512,128]{1,0:T(8,128)S(1)} %get-tuple-element.16), channel_id=1, source_target_pairs={{0,2},{2,0},{4,6},{6,4},{8,10},{10,8},{12,14},{14,12},{16,18},{18,... | collective-permute-start | bytes 786440 | tf_op jit(solution)/shard_map/ppermute | solution.py:407
